TPU v7x, 128 devices: a whole 4x4x4 slice. The times are simulated.
128 devices in a mesh: lon: 64 (over x, y, z), lat: 2 (over core).
Axes of the slice: x: 4, y: 4, z: 4, core: 2. Of those that a mesh axis runs over, the one named last changes fastest.
Arguments:
- right_side: float32 [3072, 16384], P('lat', 'lon'), may hold values from -26.2 to 26.2
- east_face: bfloat16 [3072, 16384], P('lat', 'lon'), may hold values from 0.5 to 2
- north_face: bfloat16 [3072, 16384], P('lat', 'lon'), may hold values from 0.5 to 2
- left_factor: bfloat16 [2, 1536, 128, 128], P('lat', 'lon'), may hold values from -0.008 to 1.8
- right_factor: bfloat16 [2, 1536, 128, 128], P('lat', 'lon'), may hold values from -0.008 to 1.8
- wet_list: int32 [2, 1536], P('lat', 'lon'), may hold values from 0 to 24, as said below
Outputs:
- solution: float32 [3072, 16384], P('lat', 'lon')
- precond_residual: bfloat16 [3072, 16384], P('lat', 'lon')
Inputs may be any that keep to these rules, and one draw needn't show every extreme that they name: `wet_list`: each device's slots hold the local indices of its wet tiles in increasing order, then 24 in the remaining slots. Some device has all 24 tiles wet. The two devices of one longitude index whose latitude indices are 2 j and 2 j + 1 hold at most 32 wet tiles together, and their counts differ by at most 16; in every draw some such pair reaches both bounds.
All inputs are finite; a program needn't handle non-finite values.
Results may differ from a plain program's by a relative error of at most 0.012.
The roundings to bfloat16 on the way count: a program that leaves them out, or rounds other values in their place, can miss the bound.
Values may be sent and summed in bfloat16 or wider, within the bound.
No kernel may reach another device: no remote copies, remote signals or barrier semaphores. Data moves between devices by JAX's collectives and lax.ppermute only.
A program may use at most 128 MiB of HBM per device.

v0:
```python
import functools

import jax
import jax.numpy as jnp
from jax import lax
from jax.experimental import pallas as pl
from jax.experimental.pallas import tpu as pltpu
from jax.sharding import PartitionSpec as P

EDGE = 128
CELLS = 2 * EDGE
surface_term = 0.0001
F32 = jnp.float32
BF16 = jnp.bfloat16
VMEM_LIMIT = 8 * 1024 * 1024
HEAD = 6
SPAN = 16
ROWS = 16


def dot(left, right):
    return jnp.dot(left, right, preferred_element_type=F32)


def dot_nt(left, right):
    return lax.dot_general(left, right, (((1,), (1,)), ((), ())), preferred_element_type=F32)


def lane_index(rows, cols):
    return lax.broadcasted_iota(jnp.int32, (rows, cols), 1)


def row_index(rows, cols):
    return lax.broadcasted_iota(jnp.int32, (rows, cols), 0)


def rounded_product(left, tile, right):
    partial = dot(left, tile).astype(BF16)
    return dot(partial, right).astype(BF16)


def split(value):
    high = value.astype(BF16)
    return high, (value - high.astype(F32)).astype(BF16)


def wide_product(left, tile, right):
    partial = dot(jnp.concatenate([left, left], axis=1), jnp.concatenate(split(tile), axis=0))
    return dot(jnp.concatenate(split(partial), axis=1), jnp.concatenate([right, right], axis=0))


def fold(block):
    total = block[0:8]
    for k in range(1, block.shape[0] // 8):
        total = total + block[8 * k : 8 * k + 8]
    return total


def total(value):
    return jnp.sum(jnp.sum(value, axis=0, keepdims=True), axis=1, keepdims=True)


def column(rows_ref, i):
    return jnp.broadcast_to(rows_ref[i : i + 1, :], (EDGE, EDGE)).T


def on_low_band():
    return lax.axis_index("lat") == 0


def on_odd_sector():
    return lax.axis_index("lon") % 2 == 1


def held_up():
    return lax.axis_index("lon") % SPAN == 0


def set_row(block, at, value):
    row = row_index(8, CELLS)
    if at == 0:
        return jnp.concatenate([jnp.where(row == 0, value, block[:8]), block[8:]], axis=0)
    return jnp.concatenate([block[:-8], jnp.where(row == 7, value, block[-8:])], axis=0)


def differences(i, tile_rows, field_ref, wet_ref):
    field = field_ref[i * EDGE : (i + 1) * EDGE, :]
    wet = wet_ref[i : i + 1, :]
    lane = lane_index(1, CELLS)
    both = wet * pltpu.roll(wet, EDGE, 1)
    east_wet = jnp.where(lane == EDGE - 1, both, jnp.where(lane == CELLS - 1, 0.0, 1.0))
    above = min((i + 1) * EDGE, tile_rows * EDGE - 1)
    north = set_row(pltpu.roll(field, EDGE - 1, 0), -1, field_ref[above : above + 1, :])
    north_wet = wet * wet_ref[i + 1 : i + 2, :]
    return field, field - pltpu.roll(field, CELLS - 1, 1), field - north, east_wet, north_wet


def stencil(i, tile_rows, field_ref, ef_ref, nf_ref, wet_ref, south_flux, top_flux):
    rows = slice(i * EDGE, (i + 1) * EDGE)
    field, over_e, over_n, east_wet, north_wet = differences(i, tile_rows, field_ref, wet_ref)
    flux_e = (ef_ref[rows, :].astype(F32) * east_wet) * over_e
    flux_n = nf_ref[rows, :].astype(F32) * over_n
    last = top_flux if i == tile_rows - 1 else flux_n[EDGE - 1 :, :] * north_wet
    flux_n = set_row(flux_n, -1, last)
    flux_s = set_row(pltpu.roll(flux_n, 1, 0), 0, south_flux)
    image = surface_term * field + (flux_e - pltpu.roll(flux_e, 1, 1)) + (flux_n - flux_s)
    return field, image, last


def lat_flux(coef, own, other):
    flux = coef * (own - other)
    low = on_low_band()
    return jnp.where(low, flux, 0.0), jnp.where(low, 0.0, -flux)


def edge_rows(i, block, east_ref, west_ref):
    west_ref[i : i + 1, :] = block[:, :EDGE].T[0:1, :]
    east_ref[i : i + 1, :] = block[:, EDGE:].T[EDGE - 1 :, :]


def boundary_row(ref):
    return jnp.where(on_low_band(), ref[ref.shape[0] - 1 :, :], ref[0:1, :])


def first_kernel(
    wet_hbm, rhs_hbm, left_hbm, right_hbm, ef_hbm, nf_hbm,
    z_ref, short_ref, rhs_ref, left_ref, right_ref, ef_ref, nf_ref, wet_ref, to_e, to_w, to_a, to_b, to_l, sum_ref,
    list_ref, flags_ref, sems,
):
    tile_rows = rhs_hbm.shape[0] // EDGE
    tiles = 2 * tile_rows
    used = [0]

    def load(source, target):
        copy = pltpu.make_async_copy(source, target, sems.at[used[0]])
        used[0] += 1
        copy.start()
        return copy

    listing = load(wet_hbm, list_ref)
    loads = {}
    for at, stop in ((0, HEAD), (HEAD, tile_rows)):
        rows, some = pl.ds(at * EDGE, (stop - at) * EDGE), pl.ds(at, stop - at)
        loads[at] = [
            load(rhs_hbm.at[rows], rhs_ref.at[rows]),
            load(left_hbm.at[some], left_ref.at[some]),
            load(right_hbm.at[some], right_ref.at[some]),
        ]
    faces = [load(ef_hbm, ef_ref), load(nf_hbm, nf_ref)]
    for ref in (wet_ref, to_e, to_w, to_l):
        ref[...] = jnp.zeros_like(ref)
    listing.wait()
    for t in range(flags_ref.shape[0]):
        flags_ref[t] = 0.0
    for k in range(tiles):
        flags_ref[list_ref[0, k]] = 1.0
    lane = lane_index(1, CELLS)
    for i in range(tile_rows):
        wet_ref[i : i + 1, :] = jnp.where(lane < EDGE, flags_ref[2 * i], flags_ref[2 * i + 1])
    sums = jnp.zeros(sum_ref.shape, F32)
    for i in range(tile_rows):
        for copy in loads.get(i, ()):
            copy.wait()
        rows = slice(i * EDGE, (i + 1) * EDGE)
        residual = rhs_ref[rows, :] * wet_ref[i : i + 1, :]
        rounded = residual.astype(BF16)
        parts = [
            rounded_product(left_ref[i, k], rounded[:, k * EDGE : (k + 1) * EDGE], right_ref[i, k]) for k in range(2)
        ]
        short = jnp.concatenate(parts, axis=1)
        short_ref[rows, :] = short
        precond = short.astype(F32)
        z_ref[rows, :] = precond
        edge_rows(i, precond, to_e, to_w)
        sums = sums + fold(residual * precond)
    sum_ref[...] = sums
    for copy in faces:
        copy.wait()
    for i in range(tile_rows):
        face = ef_ref[i * EDGE : (i + 1) * EDGE, EDGE:].astype(F32).T[EDGE - 1 :, :]
        to_e[ROWS + i : ROWS + i + 1, :] = face * wet_ref[i : i + 1, EDGE:]
    to_w[ROWS : ROWS + tile_rows, :] = wet_ref[:tile_rows, :EDGE]
    to_l[0:1, :] = boundary_row(z_ref)
    rows = tile_rows * EDGE
    last = nf_ref[rows - 16 : rows, :].astype(F32)[15:16, :] * wet_ref[tile_rows - 1 : tile_rows, :]
    to_l[1:2, :] = jnp.where(on_low_band(), last, wet_ref[0:1, :])
    odd = on_odd_sector()
    to_a[...] = jnp.where(odd, to_e[...], to_w[...])
    to_b[...] = jnp.where(odd, to_w[...], to_e[...])


def inner(z_ref, left_ref, right_ref, ef_ref, nf_ref, wet_ref, q_ref, w_ref, east_ref, west_ref):
    tile_rows = z_ref.shape[0] // EDGE
    east_ref[...] = jnp.zeros_like(east_ref)
    west_ref[...] = jnp.zeros_like(west_ref)
    south = top = jnp.zeros((1, CELLS), F32)
    for i in range(tile_rows):
        rows = slice(i * EDGE, (i + 1) * EDGE)
        _, image, south = stencil(i, tile_rows, z_ref, ef_ref, nf_ref, wet_ref, south, top)
        q_ref[rows, :] = image
        parts = [
            wide_product(left_ref[i, k], image[:, k * EDGE : (k + 1) * EDGE], right_ref[i, k]) for k in range(2)
        ]
        product = jnp.concatenate(parts, axis=1)
        w_ref[rows, :] = product
        edge_rows(i, product, east_ref, west_ref)


def early_inner_kernel(a_in, b_in, *refs):
    *arrays, to_a, to_b = refs
    to_a[...] = a_in[...]
    to_b[...] = b_in[...]

    @pl.when(held_up())
    def _():
        inner(*arrays)


def late_inner_kernel(*refs):
    @pl.when(jnp.logical_not(held_up()))
    def _():
        inner(*refs)


def lat_kernel(early_w, late_w, left_ref, right_ref, to_l, in_l, lat_ref, row_e, row_w):
    tile_rows = early_w.shape[0] // EDGE
    low = on_low_band()
    end = tile_rows - 1
    flux = to_l[1:2, :] * in_l[1:2, :] * (to_l[0:1, :] - in_l[0:1, :])
    pick = (lane_index(16, EDGE) == jnp.where(low, EDGE - 1, 0)) & (row_index(16, EDGE) == 0)
    pick = jnp.where(pick, 1.0, 0.0).astype(BF16)
    boundary = jnp.where(held_up(), boundary_row(early_w), boundary_row(late_w))
    for ref in (lat_ref, row_e, row_w):
        ref[...] = jnp.zeros_like(ref)
    for k in range(2):
        at = slice(k * EDGE, (k + 1) * EDGE)
        left = jnp.where(low, left_ref[end, k], left_ref[0, k])
        right = jnp.where(low, right_ref[end, k], right_ref[0, k])
        by_col = dot_nt(pick, left)[0:1, :]
        by_row = dot(jnp.concatenate(split(jnp.broadcast_to(flux[:, at], (16, EDGE))), axis=0), right)
        by_row = by_row[0:1, :] + by_row[16:17, :]
        lat_ref[0:1, at] = by_col
        lat_ref[1:2, at] = by_row
        lat_ref[3:4, at] = boundary[:, at] + jnp.where(low, by_col[:, EDGE - 1 :], by_col[:, 0:1]) * by_row
    lat_ref[2:3, :] = flux
    for i in range(tile_rows):
        row_e[i : i + 1, :] = right_ref[i, 1, EDGE - 16 :, :].astype(F32)[15:16, :]
        row_w[i : i + 1, :] = right_ref[i, 0, 0:16, :].astype(F32)[0:1, :]


def one_side(side, left_ref, lat_ref, row_ref, early_rows, late_rows, own, in_b, in_a, edge_ref, coef, flux, turn):
    tile_rows = left_ref.shape[0]
    at = slice(side * EDGE, (side + 1) * EDGE)
    rim = side * (EDGE - 1)
    odd = on_odd_sector()
    other = jnp.where(odd, in_a[...], in_b[...]) if side else jnp.where(odd, in_b[...], in_a[...])
    coef[...] = own[ROWS:, :] * other[ROWS:, :]
    flux[...] = coef[...] * (own[:ROWS, :] - other[:ROWS, :])
    turn[...] = jnp.zeros_like(turn)
    spread = jnp.concatenate(split(flux[...]), axis=0)
    for i in range(tile_rows):
        turned = dot_nt(spread, left_ref[i, side])
        turn[i : i + 1, :] = turned[i : i + 1, :] + turned[ROWS + i : ROWS + i + 1, :]
    here = row_index(ROWS, EDGE) == jnp.where(on_low_band(), tile_rows - 1, 0)
    by_lat = lat_ref[0:1, at] * lat_ref[1:2, at][:, rim : rim + 1]
    rows = jnp.where(held_up(), early_rows[...], late_rows[...]) + jnp.where(here, by_lat, 0.0)
    edge_ref[...] = rows + turn[...] * row_ref[:, rim : rim + 1]


def edge_kernel(
    left_ref, lat_ref, row_e, row_w, early_e, late_e, early_w, late_w, to_e, to_w, in_b, in_a,
    east_ref, coef_e, flux_e, turn_e, west_ref, coef_w, flux_w, turn_w, to_l2,
):
    one_side(1, left_ref, lat_ref, row_e, early_e, late_e, to_e, in_b, in_a, east_ref, coef_e, flux_e, turn_e)
    one_side(0, left_ref, lat_ref, row_w, early_w, late_w, to_w, in_b, in_a, west_ref, coef_w, flux_w, turn_w)
    end = left_ref.shape[0] - 1
    low = on_low_band()
    by_lon = [
        jnp.where(low, turn[end : end + 1, EDGE - 1 :] * row[end : end + 1, :], turn[0:1, 0:1] * row[0:1, :])
        for turn, row in ((turn_w, row_w), (turn_e, row_e))
    ]
    to_l2[...] = jnp.zeros_like(to_l2)
    to_l2[0:1, :] = lat_ref[3:4, :] + jnp.concatenate(by_lon, axis=1)


def middle(
    z_ref, rhs_ref, q_ref, w_in, ef_ref, nf_ref, wet_ref, lat_ref, turn_e, turn_w, right_e, right_w, sum_in, w_ref, sums_ref
):
    tile_rows = z_ref.shape[0] // EDGE
    zero = jnp.zeros((8, CELLS), F32)
    zq, rw, qw, faces, squares = zero, zero, zero, zero, zero

    def complete(i, zq, rw, qw):
        rows = slice(i * EDGE, (i + 1) * EDGE)
        image = q_ref[rows, :]
        product = w_in[rows, :] + jnp.concatenate(
            [column(turn_w, i) * right_w[i : i + 1, :], column(turn_e, i) * right_e[i : i + 1, :]], axis=1
        )
        if i in (0, tile_rows - 1):
            here = on_low_band() == (i > 0)
            by_row = jnp.where(here, lat_ref[1:2, :], 0.0)
            by_col = [jnp.broadcast_to(lat_ref[0:1, k * EDGE : (k + 1) * EDGE], (EDGE, EDGE)).T for k in range(2)]
            product = product + jnp.concatenate(by_col, axis=1) * by_row
        w_ref[rows, :] = product
        return zq + fold(z_ref[rows, :] * image), rw + fold(rhs_ref[rows, :] * product), qw + fold(image * product)

    zq, rw, qw = complete(0, zq, rw, qw)
    for i in range(tile_rows):
        if i + 1 < tile_rows:
            zq, rw, qw = complete(i + 1, zq, rw, qw)
        rows = slice(i * EDGE, (i + 1) * EDGE)
        field, over_e, over_n, east_wet, north_wet = differences(i, tile_rows, w_ref, wet_ref)
        by_e = ef_ref[rows, :].astype(F32) * east_wet * (over_e * over_e)
        by_n = nf_ref[rows, :].astype(F32) * (over_n * over_n)
        by_n = set_row(by_n, -1, 0.0 if i == tile_rows - 1 else by_n[EDGE - 1 :, :] * north_wet)
        faces = faces + fold(by_e + by_n)
        squares = squares + fold(field * field)
    for k, total in enumerate((sum_in[...], zq, rw, qw, faces + surface_term * squares)):
        sums_ref[k] = total


def early_middle_kernel(west_in, *refs):
    *arrays, to_w = refs
    to_w[...] = west_in[...]

    @pl.when(held_up())
    def _():
        middle(*arrays)


def late_middle_kernel(early_w, early_sums, *refs):
    w_ref, sums_ref = refs[-2:]
    early = held_up()

    @pl.when(early)
    def _():
        w_ref[...] = early_w[...]
        sums_ref[...] = early_sums[...]

    @pl.when(jnp.logical_not(early))
    def _():
        middle(*refs)


def sums_kernel(
    sums_in, east_ref, west_ref, to_e, to_w, lat_ref, flux_e1, flux_w1, coef_w, own_l, own_l2, in_l, from_w, in_l2,
    packed_ref, flux_w, flux_l,
):
    over_w = west_ref[...] - from_w[...]
    flux_w[...] = coef_w[...] * over_w
    top, bottom = lat_flux(own_l[1:2, :] * in_l[1:2, :], own_l2[0:1, :], in_l2[0:1, :])
    flux_l[...] = jnp.zeros_like(flux_l)
    flux_l[0:1, :] = top
    flux_l[1:2, :] = -bottom

    outer = {
        1: total(flux_e1[...] * to_e[:ROWS, :] + flux_w1[...] * to_w[:ROWS, :])
        + total(lat_ref[2:3, :] * own_l[0:1, :]),
        3: total(flux_e1[...] * east_ref[...] + flux_w1[...] * west_ref[...])
        + total(lat_ref[2:3, :] * own_l2[0:1, :]),
        4: total(flux_w[...] * over_w) + total((top - bottom) * own_l2[0:1, :]),
    }
    lane = lane_index(1, EDGE)
    packed = jnp.zeros((1, EDGE), F32)
    for k in range(5):
        value = total(sums_in[k])
        packed = jnp.where(lane == k, value + outer[k] if k in outer else value, packed)
    packed_ref[...] = jnp.broadcast_to(packed, packed_ref.shape)


def outer_kernel(
    left_hbm, right_hbm, ef_hbm, nf_hbm, w_ref, wet_ref, east_ref, coef_e, from_e, flux_w, flux_l, sums_ref,
    u_ref, share_ref, left_ref, right_ref, ef_ref, nf_ref, flux_e, sems,
):
    tile_rows = w_ref.shape[0] // EDGE
    step = tile_rows // 2
    loads = []
    for k in range(tile_rows // step):
        rows, some = pl.ds(k * step * EDGE, step * EDGE), pl.ds(k * step, step)
        group = [
            pltpu.make_async_copy(source.at[place], target.at[place], sems.at[4 * k + n])
            for n, (source, target, place) in enumerate(
                ((ef_hbm, ef_ref, rows), (nf_hbm, nf_ref, rows), (left_hbm, left_ref, some), (right_hbm, right_ref, some))
            )
        ]
        for copy in group:
            copy.start()
        loads.append(group)
    flux_e[...] = coef_e[...] * (east_ref[...] - from_e[...])
    lane = lane_index(EDGE, EDGE)
    south, top = -flux_l[1:2, :], flux_l[0:1, :]
    zq, qw = (total(sums_ref[k]) for k in (1, 3))
    share = jnp.where(zq > 0.0, qw / jnp.where(zq > 0.0, zq, 1.0), 0.0)
    share_ref[...] = jnp.broadcast_to(share, share_ref.shape)
    for i in range(tile_rows):
        if i % step == 0:
            for copy in loads[i // step]:
                copy.wait()
        _, image, south = stencil(i, tile_rows, w_ref, ef_ref, nf_ref, wet_ref, south, top)
        image = image + jnp.concatenate(
            [jnp.where(lane == 0, column(flux_w, i), 0.0), jnp.where(lane == EDGE - 1, column(flux_e, i), 0.0)], axis=1
        )
        parts = [
            wide_product(left_ref[i, k], image[:, k * EDGE : (k + 1) * EDGE], right_ref[i, k]) for k in range(2)
        ]
        rows = slice(i * EDGE, (i + 1) * EDGE)
        u_ref[rows, :] = (jnp.concatenate(parts, axis=1) - share * w_ref[rows, :]).astype(BF16)


def last_kernel(all_ref, z_ref, w_ref, u_ref, share_ref, sol_hbm, pre_hbm, sol_ref, pre_ref, sems):
    tile_rows = z_ref.shape[0] // EDGE
    totals = jnp.sum(all_ref[...], axis=0, keepdims=True)
    lane = lane_index(1, EDGE)
    rz, zq, rw, qw, waw = (jnp.sum(jnp.where(lane == k, totals, 0.0), axis=1, keepdims=True) for k in range(5))
    step0 = rz / zq
    rz1 = step0 * (step0 * qw - rw)
    grow = 1.0 + rz1 / rz
    step1 = rz1 / (grow * grow * zq - 2.0 * grow * step0 * qw + step0 * step0 * waw)
    with_z = step0 + step1 * grow
    with_w = -step1 * step0
    less_w = with_z + with_w * share_ref[0:1, 0:1]
    group = 2 * EDGE
    stores = []
    for i in range(tile_rows * EDGE // group):
        rows = slice(i * group, (i + 1) * group)
        precond, product = z_ref[rows, :].astype(F32), w_ref[rows, :]
        sol_ref[rows, :] = with_z * precond + with_w * product
        pre_ref[rows, :] = (precond - less_w * product - with_w * u_ref[rows, :].astype(F32)).astype(BF16)
        place = pl.ds(i * group, group)
        for k, (source, target) in enumerate(((sol_ref, sol_hbm), (pre_ref, pre_hbm))):
            copy = pltpu.make_async_copy(source.at[place], target.at[place], sems.at[2 * i + k])
            copy.start()
            stores.append(copy)
    for copy in stores:
        copy.wait()


def call(kernel, outs, args, name, scratch=(), in_space=pltpu.VMEM, out_space=pltpu.VMEM, flops=0):
    if not isinstance(in_space, list):
        in_space = [in_space] * len(args)
    return pl.pallas_call(
        kernel,
        out_shape=outs,
        in_specs=[pl.BlockSpec(memory_space=space) for space in in_space],
        out_specs=[pl.BlockSpec(memory_space=out_space)] * len(outs),
        scratch_shapes=scratch,
        compiler_params=pltpu.CompilerParams(vmem_limit_bytes=VMEM_LIMIT),
        cost_estimate=pl.CostEstimate(flops=flops, bytes_accessed=0, transcendentals=0),
        name=name,
    )(*args)


def per_device(right_side, east_face, north_face, left_factor, right_factor, wet_list):
    rows, cols = right_side.shape
    lons, lats = lax.axis_size("lon"), lax.axis_size("lat")
    tile_rows = rows // EDGE
    shape = functools.partial(jax.ShapeDtypeStruct, dtype=F32)
    like = lambda a: jax.ShapeDtypeStruct(a.shape, a.dtype)
    field = shape((rows, cols))
    half = jax.ShapeDtypeStruct((rows, cols), BF16)
    edge = shape((ROWS, EDGE))
    message = shape((2 * ROWS, EDGE))
    strip = shape((8, cols))
    across = [(0, 1), (1, 0)]

    def pairs(parity):
        forward = [(i, (i + 1) % lons) for i in range(parity, lons, 2)]
        return forward + [(b, a) for a, b in forward]

    by_place = (tile_rows, 2, EDGE, EDGE)
    left_factor, right_factor = left_factor.reshape(by_place), right_factor.reshape(by_place)
    arguments = [
        pltpu.with_memory_space_constraint(a, pltpu.HBM)
        for a in (wet_list, right_side, left_factor, right_factor, east_face, north_face)
    ]
    z, short, rhs, left, right, ef, nf, wet, to_e, to_w, to_a, to_b, to_l, rz = call(
        first_kernel,
        [field, half, field, like(left_factor), like(right_factor), like(east_face), like(north_face),
         shape((ROWS, cols)), message, message, message, message, strip, strip],
        arguments, "first",
        [pltpu.SMEM(wet_list.shape, jnp.int32), pltpu.SMEM((32,), F32),
         pltpu.SemaphoreType.DMA((9,))],
        in_space=pltpu.HBM,
    )
    arrays = (z, left, right, ef, nf, wet)
    results = [field, field, edge, edge]
    *early, far_a, far_b = call(early_inner_kernel, results + [message, message], (to_a, to_b, *arrays), "early_inner")
    in_b = lax.ppermute(far_b, "lon", pairs(0))
    in_a = lax.ppermute(far_a, "lon", pairs(1))
    in_l = lax.ppermute(to_l, "lat", across)
    late = call(late_inner_kernel, results, arrays, "late_inner")
    lat, row_e, row_w = call(
        lat_kernel, [strip, edge, edge], (early[1], late[1], left, right, to_l, in_l), "lat"
    )
    east, coef_e, flux_e1, turn_e, west, coef_w, flux_w1, turn_w, to_l2 = call(
        edge_kernel, [edge] * 8 + [strip],
        (left, lat, row_e, row_w, early[2], late[2], early[3], late[3], to_e, to_w, in_b, in_a), "edges",
    )
    from_w2 = lax.ppermute(east, "lon", [(i, (i + 1) % lons) for i in range(lons)])
    in_l2 = lax.ppermute(to_l2, "lat", across)
    results = [field, shape((5, 8, cols))]
    faces = (ef, nf, wet, lat, turn_e, turn_w, row_e, row_w, rz)
    *done, to_w2 = call(early_middle_kernel, results + [edge], (west, z, rhs, *early[:2], *faces), "early_middle")
    from_e2 = lax.ppermute(to_w2, "lon", [((i + 1) % lons, i) for i in range(lons)])
    w, sums = call(late_middle_kernel, results, (*done, z, rhs, *late[:2], *faces), "late_middle")
    packed, flux_w, flux_l = call(
        sums_kernel, [shape((lons * lats, EDGE)), edge, strip],
        (sums, east, west, to_e, to_w, lat, flux_e1, flux_w1, coef_w, to_l, to_l2, in_l, from_w2, in_l2), "sums",
    )
    everyone = lax.all_to_all(packed, ("lon", "lat"), 0, 0, tiled=True)
    u, share = call(
        outer_kernel, [half, shape((8, EDGE))],
        (*arguments[2:], w, wet, east, coef_e, from_e2, flux_w, flux_l, sums), "outer",
        [pltpu.VMEM(a.shape, a.dtype) for a in arguments[2:]]
        + [pltpu.VMEM((ROWS, EDGE), F32), pltpu.SemaphoreType.DMA((8,))],
        in_space=[pltpu.HBM] * 4 + [pltpu.VMEM] * 8, flops=100_000_000_000,
    )
    return tuple(
        call(
            last_kernel, [field, half], (everyone, short, w, u, share), "last",
            [pltpu.VMEM((rows, cols), F32), pltpu.VMEM((rows, cols), BF16), pltpu.SemaphoreType.DMA((tile_rows,))],
            out_space=pltpu.HBM,
        )
    )


def solution(mesh):
    tiles = P("lat", "lon", None, None)
    cells = P("lat", "lon")
    return jax.shard_map(
        per_device,
        mesh=mesh,
        in_specs=(cells, cells, cells, tiles, tiles, cells),
        out_specs=(cells, cells),
        check_vma=False,
    )
```

profile of v0, /device:TPU:1, one launch (start us, length us, event | category | flops | bytes accessed | tf_op | source)
XLA Modules:
  0.0 41.5 jit_solution(17993901717105256285)
XLA Ops:
  0.6 2.7 %first.1 = (f32[1536,256]{1,0:T(8,128)S(1)}, bf16[1536,256]{1,0:T(8,128)(2,1)S(1)}, f32[1536,256]{1,0:T(8,128)S(1)}, bf16[12,2,128,128]{3,2,1,0:T(8,128)(2,1)S(1...) custom-call(s32[1,24]{1,0:T(1,128)} %wet_hbm.1, ...), custom_call_target="tpu_custom_call" | custom-call | tf_op jit(solution)/shard_map/first/pallas_call | solution.py:441
  3.4 2.1 %early_inner.1 = (f32[1536,256]{1,0:T(8,128)S(1)}, f32[1536,256]{1,0:T(8,128)S(1)}, f32[16,128]{1,0:T(8,128)S(1)}, f32[16,128]{1,0:T(8,128)S(1)}, f32[32,128]{1,0:T(8,128)S(1)}, /*index=5*/f32[32,128]{1,0:T(8,128)S(1)}) custom-call(f32[32,128]{1,0:T(8,128)S(1)} %get-tuple-element.49.a_in, f32[32,128]{1,0:T(8,128)S(1)} %get-tuple-element.50.b_in, ...), custom_call_target="tpu_custom_call" | custom-call | tf_op jit(solution)/shard_map/early_inner/pallas_call | solution.py:441
  5.5 0.4 %collective-permute-start.1 = (f32[32,128]{1,0:T(8,128)S(1)}, f32[32,128]{1,0:T(8,128)S(1)}, u32[]{:S(2)}, u32[]{:S(2)}) collective-permute-start(f32[32,128]{1,0:T(8,128)S(1)} %get-tuple-element.68), channel_id=1, source_target_pairs={{0,2},{4,6},{8,10},{12,14},{16,18},{20,22},{24,26},{28,30},{32,34}... | collective-permute-start | bytes 49160 | tf_op jit(solution)/shard_map/ppermute | solution.py:488
  5.9 6.9 %collective-permute-start.2 = (f32[32,128]{1,0:T(8,128)S(1)}, f32[32,128]{1,0:T(8,128)S(1)}, u32[]{:S(2)}, u32[]{:S(2)}) collective-permute-start(f32[32,128]{1,0:T(8,128)S(1)} %get-tuple-element.69), channel_id=1, source_target_pairs={{2,4},{6,8},{10,12},{14,16},{18,20},{22,24},{26,28},{30,32},{34,36... | collective-permute-start | bytes 49160 | tf_op jit(solution)/shard_map/ppermute | solution.py:489
  12.8 1.2 %collective-permute-start = (f32[8,256]{1,0:T(8,128)S(1)}, f32[8,256]{1,0:T(8,128)S(1)}, u32[]{:S(2)}, u32[]{:S(2)}) collective-permute-start(f32[8,256]{1,0:T(8,128)S(1)} %get-tuple-element.58.to_l.own_l), channel_id=1, source_target_pairs={{0,1},{1,0},{2,3},{3,2},{4,5},{5,4},{6,7},{7,6},{8,9},{9,8},{10,11... | collective-permute-start | bytes 24584 | tf_op jit(solution)/shard_map/ppermute | solution.py:490
  14.1 0.8 %collective-permute-done.in_l = f32[8,256]{1,0:T(8,128)S(1)} collective-permute-done((f32[8,256]{1,0:T(8,128)S(1)}, f32[8,256]{1,0:T(8,128)S(1)}, u32[]{:S(2)}, u32[]{:S(2)}) %collective-permute-start) | collective-permute-done | bytes 8224 | tf_op jit(solution)/shard_map/ppermute | solution.py:490
  14.9 0.3 lat.1
  15.2 0.0 collective-permute-done.1.in_b
  15.2 0.0 collective-permute-done.2.in_a
  15.2 0.6 %edges.1 = (f32[16,128]{1,0:T(8,128)S(1)}, f32[16,128]{1,0:T(8,128)S(1)}, f32[16,128]{1,0:T(8,128)S(1)}, f32[16,128]{1,0:T(8,128)S(1)}, f32[16,128]{1,0:T(8,128)...) custom-call(bf16[12,2,128,128]{3,2,1,0:T(8,128)(2,1)S(1)} %get-tuple-element, ...), custom_call_target="tpu_custom_call" | custom-call | tf_op jit(solution)/shard_map/edges/pallas_call | solution.py:441
  15.8 1.1 %collective-permute-start.4 = (f32[8,256]{1,0:T(8,128)S(1)}, f32[8,256]{1,0:T(8,128)S(1)}, u32[]{:S(2)}, u32[]{:S(2)}) collective-permute-start(f32[8,256]{1,0:T(8,128)S(1)} %get-tuple-element.84.own_l2), channel_id=1, source_target_pairs={{0,1},{1,0},{2,3},{3,2},{4,5},{5,4},{6,7},{7,6},{8,9},{9,8},{10,11... | collective-permute-start | bytes 24584 | tf_op jit(solution)/shard_map/ppermute | solution.py:500
  16.9 0.0 collective-permute-start.3
  16.9 1.5 %early_middle.1 = (f32[1536,256]{1,0:T(8,128)S(1)}, f32[5,8,256]{2,1,0:T(8,128)S(1)}, f32[16,128]{1,0:T(8,128)S(1)}) custom-call(f32[16,128]{1,0:T(8,128)S(1)} %get-tuple-element.70.west_in.west_ref, f32[1536,256]{1,0:T(8,128)S(1)} %get-tuple-element.51.refs_0_, f32[1536,256]{1,0:T(8,128)S(1)} %get-tuple-element.71.refs_1_, ...), custom_call_target="tpu_custom_call" | custom-call | tf_op jit(solution)/shard_map/early_middle/pallas_call | solution.py:441
  18.4 5.4 %collective-permute-start.5 = (f32[16,128]{1,0:T(8,128)S(1)}, f32[16,128]{1,0:T(8,128)S(1)}, u32[]{:S(2)}, u32[]{:S(2)}) collective-permute-start(f32[16,128]{1,0:T(8,128)S(1)} %get-tuple-element.89), channel_id=1, source_target_pairs={{2,0},{4,2},{6,4},{8,6},{10,8},{12,10},{14,12},{16,14},{18,16},{20... | collective-permute-start | bytes 24584 | tf_op jit(solution)/shard_map/ppermute | solution.py:504
  23.8 0.1 late_middle.1
  23.9 0.0 collective-permute-done.4.in_l2
  23.9 0.9 %collective-permute-done.3.from_w = f32[16,128]{1,0:T(8,128)S(1)} collective-permute-done((f32[16,128]{1,0:T(8,128)S(1)}, f32[16,128]{1,0:T(8,128)S(1)}, u32[]{:S(2)}, u32[]{:S(2)}) %collective-permute-start.3) | collective-permute-done | bytes 8224 | tf_op jit(solution)/shard_map/ppermute | solution.py:499
  24.9 0.7 %sums.1 = (f32[128,128]{1,0:T(8,128)}, f32[16,128]{1,0:T(8,128)S(1)}, f32[8,256]{1,0:T(8,128)S(1)}) custom-call(f32[5,8,256]{2,1,0:T(8,128)S(1)} %get-tuple-element.79.sums_in.sums_ref, f32[16,128]{1,0:T(8,128)S(1)} %get-tuple-element.80.east_ref, f32[16,128]{1,0:T(8,128)S(1)} %get-tuple-element.70.west_in.west_ref, f32[32,128]{1,0:T(8,128)S(1)} %get-tuple-element.66.to_e, ...), custom_call_target="tpu_custom_call" | custom-call | tf_op jit(solution)/shard_map/sums/pallas_call | solution.py:441
  25.6 4.6 %all-to-all-start = ((f32[128,1,128]{2,1,0:T(1,128)}), f32[128,1,128]{2,1,0:T(1,128)S(1)}, u32[]{:S(2)}, u32[]{:S(2)}) async-start(f32[128,1,128]{2,1,0:T(1,128)} %bitcast.3), calls=%async_computation | async-start | bytes 131072 | tf_op jit(solution)/shard_map/all_to_all | solution.py:510
  30.2 0.0 collective-permute-done.5.from_e
  30.2 4.2 %outer.1 = (bf16[1536,256]{1,0:T(8,128)(2,1)S(1)}, f32[8,128]{1,0:T(8,128)S(1)}) custom-call(bf16[12,2,128,128]{3,2,1,0:T(8,128)(2,1)} %bitcast.8, bf16[12,2,128,128]{3,2,1,0:T(8,128)(2,1)} %bitcast.10, bf16[1536,256]{1,0:T(8,128)(2,1)} %ef_hbm.3, bf16[1536,256]{1,0:T(8,128)(2,1)} %nf_hbm.3, f32[1536,256]{1,0:T(8,128)S(1)} %get-tuple-element.87.w_ref, ...), custom_call_target="tpu_custom_call" | custom-call | flops 99999997952 | tf_op jit(solution)/shard_map/outer/pallas_call | solution.py:441
  34.5 5.2 %all-to-all-done = f32[128,1,128]{2,1,0:T(1,128)S(1)} async-done(((f32[128,1,128]{2,1,0:T(1,128)}), f32[128,1,128]{2,1,0:T(1,128)S(1)}, u32[]{:S(2)}, u32[]{:S(2)}) %all-to-all-start) | async-done | bytes 65568 | tf_op jit(solution)/shard_map/all_to_all | solution.py:510
  39.6 1.7 %last.1 = (f32[1536,256]{1,0:T(8,128)}, bf16[1536,256]{1,0:T(8,128)(2,1)}) custom-call(f32[128,128]{1,0:T(8,128)S(1)} %bitcast.6, bf16[1536,256]{1,0:T(8,128)(2,1)S(1)} %get-tuple-element.86.z_ref, f32[1536,256]{1,0:T(8,128)S(1)} %get-tuple-element.87.w_ref, bf16[1536,256]{1,0:T(8,128)(2,1)S(1)} %get-tuple-element.92.u_ref, ...), custom_call_target="tpu_custom_call" | custom-call | tf_op jit(solution)/shard_map/last/pallas_call | solution.py:441
  (1 shorter events, 0.0 us)
Async XLA Ops:
  5.5 9.7 %collective-permute-start.1 = (f32[32,128]{1,0:T(8,128)S(1)}, f32[32,128]{1,0:T(8,128)S(1)}, u32[]{:S(2)}, u32[]{:S(2)}) collective-permute-start(f32[32,128]{1,0:T(8,128)S(1)} %get-tuple-element.68), channel_id=1, source_target_pairs={{0,2},{4,6},{8,10},{12,14},{16,18},{20,22},{24,26},{28,30},{32,34}... | collective-permute-start | bytes 49160 | tf_op jit(solution)/shard_map/ppermute | solution.py:488
  5.9 9.3 %collective-permute-start.2 = (f32[32,128]{1,0:T(8,128)S(1)}, f32[32,128]{1,0:T(8,128)S(1)}, u32[]{:S(2)}, u32[]{:S(2)}) collective-permute-start(f32[32,128]{1,0:T(8,128)S(1)} %get-tuple-element.69), channel_id=1, source_target_pairs={{2,4},{6,8},{10,12},{14,16},{18,20},{22,24},{26,28},{30,32},{34,36... | collective-permute-start | bytes 49160 | tf_op jit(solution)/shard_map/ppermute | solution.py:489
  12.8 2.1 %collective-permute-start = (f32[8,256]{1,0:T(8,128)S(1)}, f32[8,256]{1,0:T(8,128)S(1)}, u32[]{:S(2)}, u32[]{:S(2)}) collective-permute-start(f32[8,256]{1,0:T(8,128)S(1)} %get-tuple-element.58.to_l.own_l), channel_id=1, source_target_pairs={{0,1},{1,0},{2,3},{3,2},{4,5},{5,4},{6,7},{7,6},{8,9},{9,8},{10,11... | collective-permute-start | bytes 24584 | tf_op jit(solution)/shard_map/ppermute | solution.py:490
  15.8 8.2 %collective-permute-start.4 = (f32[8,256]{1,0:T(8,128)S(1)}, f32[8,256]{1,0:T(8,128)S(1)}, u32[]{:S(2)}, u32[]{:S(2)}) collective-permute-start(f32[8,256]{1,0:T(8,128)S(1)} %get-tuple-element.84.own_l2), channel_id=1, source_target_pairs={{0,1},{1,0},{2,3},{3,2},{4,5},{5,4},{6,7},{7,6},{8,9},{9,8},{10,11... | collective-permute-start | bytes 24584 | tf_op jit(solution)/shard_map/ppermute | solution.py:500
  16.9 7.9 %collective-permute-start.3 = (f32[16,128]{1,0:T(8,128)S(1)}, f32[16,128]{1,0:T(8,128)S(1)}, u32[]{:S(2)}, u32[]{:S(2)}) collective-permute-start(f32[16,128]{1,0:T(8,128)S(1)} %get-tuple-element.80.east_ref), channel_id=1, source_target_pairs={{0,2},{2,4},{4,6},{6,8},{8,10},{10,12},{12,14},{14,16},{16,18},{18... | collective-permute-start | bytes 24584 | tf_op jit(solution)/shard_map/ppermute | solution.py:499
  18.4 11.8 %collective-permute-start.5 = (f32[16,128]{1,0:T(8,128)S(1)}, f32[16,128]{1,0:T(8,128)S(1)}, u32[]{:S(2)}, u32[]{:S(2)}) collective-permute-start(f32[16,128]{1,0:T(8,128)S(1)} %get-tuple-element.89), channel_id=1, source_target_pairs={{2,0},{4,2},{6,4},{8,6},{10,8},{12,10},{14,12},{16,14},{18,16},{20... | collective-permute-start | bytes 24584 | tf_op jit(solution)/shard_map/ppermute | solution.py:504
  25.6 14.0 %all-to-all-start = ((f32[128,1,128]{2,1,0:T(1,128)}), f32[128,1,128]{2,1,0:T(1,128)S(1)}, u32[]{:S(2)}, u32[]{:S(2)}) async-start(f32[128,1,128]{2,1,0:T(1,128)} %bitcast.3), calls=%async_computation | async-start | bytes 131072 | tf_op jit(solution)/shard_map/all_to_all | solution.py:510
where the time goes:
time: 41.7 us; the launch traced here: 41.5 us
  starting transfers between devices  19.7 us (47%)
  Pallas kernels  14.1 us (34%)
  waiting for transfers between devices  6.9 us (17%)
  between operations  0.86 us (2%)
    pallas_call x10, Pallas kernels, call(): pl.pallas_call(kernel, out_shape=outs, in_specs=[pl.BlockSpec(memory_spac...  14.1 us
    ppermute x1, starting transfers between devices, per_device(): in_a = lax.ppermute(far_a, 'lon', pairs(1))  6.89 us
    ppermute x1, starting transfers between devices, per_device(): lax.ppermute(to_w2, 'lon', [((i + 1) % lons, i) for i in range(lons)])  5.39 us
    all_to_all x1, waiting for transfers between devices, per_device(): everyone = lax.all_to_all(packed, ('lon', 'lat'), 0, 0, tiled=True)  5.16 us
    all_to_all x1, starting transfers between devices, per_device(): everyone = lax.all_to_all(packed, ('lon', 'lat'), 0, 0, tiled=True)  4.61 us
    ppermute x1, starting transfers between devices, per_device(): in_l = lax.ppermute(to_l, 'lat', across)  1.24 us
    ppermute x1, starting transfers between devices, per_device(): in_l2 = lax.ppermute(to_l2, 'lat', across)  1.12 us
    ppermute x1, waiting for transfers between devices, per_device(): lax.ppermute(east, 'lon', [(i, (i + 1) % lons) for i in range(lons)])  0.91 us
  transfers between devices with their start and end apart: 7, of which 3 were waited for; matrix products, arithmetic and copies ran while one was open for 0% of the time, Pallas kernels for 17%

commit v1 on v0

--- a/solution.py
+++ b/solution.py
@@ -419,7 +419,7 @@
     with_z = step0 + step1 * grow
     with_w = -step1 * step0
     less_w = with_z + with_w * share_ref[0:1, 0:1]
-    group = 2 * EDGE
+    group = EDGE
     stores = []
     for i in range(tile_rows * EDGE // group):
         rows = slice(i * group, (i + 1) * group)
@@ -518,7 +518,7 @@
     return tuple(
         call(
             last_kernel, [field, half], (everyone, short, w, u, share), "last",
-            [pltpu.VMEM((rows, cols), F32), pltpu.VMEM((rows, cols), BF16), pltpu.SemaphoreType.DMA((tile_rows,))],
+            [pltpu.VMEM((rows, cols), F32), pltpu.VMEM((rows, cols), BF16), pltpu.SemaphoreType.DMA((2 * tile_rows,))],
             out_space=pltpu.HBM,
         )
     )

time: 41.7 us -> 41.7 us (level)
  no operation moved by 1% of the time
where the time goes in v1:
time: 41.7 us; the launch traced here: 41.5 us
  starting transfers between devices  19.7 us (47%)
  Pallas kernels  14.1 us (34%)
  waiting for transfers between devices  6.9 us (17%)
  between operations  0.86 us (2%)
    pallas_call x10, Pallas kernels, call(): pl.pallas_call(kernel, out_shape=outs, in_specs=[pl.BlockSpec(memory_spac...  14.1 us
    ppermute x1, starting transfers between devices, per_device(): in_a = lax.ppermute(far_a, 'lon', pairs(1))  6.89 us
    ppermute x1, starting transfers between devices, per_device(): lax.ppermute(to_w2, 'lon', [((i + 1) % lons, i) for i in range(lons)])  5.39 us
    all_to_all x1, waiting for transfers between devices, per_device(): everyone = lax.all_to_all(packed, ('lon', 'lat'), 0, 0, tiled=True)  5.16 us
    all_to_all x1, starting transfers between devices, per_device(): everyone = lax.all_to_all(packed, ('lon', 'lat'), 0, 0, tiled=True)  4.61 us
    ppermute x1, starting transfers between devices, per_device(): in_l = lax.ppermute(to_l, 'lat', across)  1.24 us
    ppermute x1, starting transfers between devices, per_device(): in_l2 = lax.ppermute(to_l2, 'lat', across)  1.12 us
    ppermute x1, waiting for transfers between devices, per_device(): lax.ppermute(east, 'lon', [(i, (i + 1) % lons) for i in range(lons)])  0.91 us
  transfers between devices with their start and end apart: 7, of which 3 were waited for; matrix products, arithmetic and copies ran while one was open for 0% of the time, Pallas kernels for 17%

profile of v1, /device:TPU:1, one launch (start us, length us, event | category | flops | bytes accessed | tf_op | source)
XLA Modules:
  0.0 41.5 jit_solution(8345608541406883443)
XLA Ops:
  0.6 2.7 %first.1 = (f32[1536,256]{1,0:T(8,128)S(1)}, bf16[1536,256]{1,0:T(8,128)(2,1)S(1)}, f32[1536,256]{1,0:T(8,128)S(1)}, bf16[12,2,128,128]{3,2,1,0:T(8,128)(2,1)S(1...) custom-call(s32[1,24]{1,0:T(1,128)} %wet_hbm.1, ...), custom_call_target="tpu_custom_call" | custom-call | tf_op jit(solution)/shard_map/first/pallas_call | solution.py:441
  3.4 2.1 %early_inner.1 = (f32[1536,256]{1,0:T(8,128)S(1)}, f32[1536,256]{1,0:T(8,128)S(1)}, f32[16,128]{1,0:T(8,128)S(1)}, f32[16,128]{1,0:T(8,128)S(1)}, f32[32,128]{1,0:T(8,128)S(1)}, /*index=5*/f32[32,128]{1,0:T(8,128)S(1)}) custom-call(f32[32,128]{1,0:T(8,128)S(1)} %get-tuple-element.49.a_in, f32[32,128]{1,0:T(8,128)S(1)} %get-tuple-element.50.b_in, ...), custom_call_target="tpu_custom_call" | custom-call | tf_op jit(solution)/shard_map/early_inner/pallas_call | solution.py:441
  5.5 0.4 %collective-permute-start.1 = (f32[32,128]{1,0:T(8,128)S(1)}, f32[32,128]{1,0:T(8,128)S(1)}, u32[]{:S(2)}, u32[]{:S(2)}) collective-permute-start(f32[32,128]{1,0:T(8,128)S(1)} %get-tuple-element.68), channel_id=1, source_target_pairs={{0,2},{4,6},{8,10},{12,14},{16,18},{20,22},{24,26},{28,30},{32,34}... | collective-permute-start | bytes 49160 | tf_op jit(solution)/shard_map/ppermute | solution.py:488
  5.9 6.9 %collective-permute-start.2 = (f32[32,128]{1,0:T(8,128)S(1)}, f32[32,128]{1,0:T(8,128)S(1)}, u32[]{:S(2)}, u32[]{:S(2)}) collective-permute-start(f32[32,128]{1,0:T(8,128)S(1)} %get-tuple-element.69), channel_id=1, source_target_pairs={{2,4},{6,8},{10,12},{14,16},{18,20},{22,24},{26,28},{30,32},{34,36... | collective-permute-start | bytes 49160 | tf_op jit(solution)/shard_map/ppermute | solution.py:489
  12.8 1.2 %collective-permute-start = (f32[8,256]{1,0:T(8,128)S(1)}, f32[8,256]{1,0:T(8,128)S(1)}, u32[]{:S(2)}, u32[]{:S(2)}) collective-permute-start(f32[8,256]{1,0:T(8,128)S(1)} %get-tuple-element.58.to_l.own_l), channel_id=1, source_target_pairs={{0,1},{1,0},{2,3},{3,2},{4,5},{5,4},{6,7},{7,6},{8,9},{9,8},{10,11... | collective-permute-start | bytes 24584 | tf_op jit(solution)/shard_map/ppermute | solution.py:490
  14.1 0.8 %collective-permute-done.in_l = f32[8,256]{1,0:T(8,128)S(1)} collective-permute-done((f32[8,256]{1,0:T(8,128)S(1)}, f32[8,256]{1,0:T(8,128)S(1)}, u32[]{:S(2)}, u32[]{:S(2)}) %collective-permute-start) | collective-permute-done | bytes 8224 | tf_op jit(solution)/shard_map/ppermute | solution.py:490
  14.9 0.3 lat.1
  15.2 0.0 collective-permute-done.1.in_b
  15.2 0.0 collective-permute-done.2.in_a
  15.2 0.6 %edges.1 = (f32[16,128]{1,0:T(8,128)S(1)}, f32[16,128]{1,0:T(8,128)S(1)}, f32[16,128]{1,0:T(8,128)S(1)}, f32[16,128]{1,0:T(8,128)S(1)}, f32[16,128]{1,0:T(8,128)...) custom-call(bf16[12,2,128,128]{3,2,1,0:T(8,128)(2,1)S(1)} %get-tuple-element, ...), custom_call_target="tpu_custom_call" | custom-call | tf_op jit(solution)/shard_map/edges/pallas_call | solution.py:441
  15.8 1.1 %collective-permute-start.4 = (f32[8,256]{1,0:T(8,128)S(1)}, f32[8,256]{1,0:T(8,128)S(1)}, u32[]{:S(2)}, u32[]{:S(2)}) collective-permute-start(f32[8,256]{1,0:T(8,128)S(1)} %get-tuple-element.84.own_l2), channel_id=1, source_target_pairs={{0,1},{1,0},{2,3},{3,2},{4,5},{5,4},{6,7},{7,6},{8,9},{9,8},{10,11... | collective-permute-start | bytes 24584 | tf_op jit(solution)/shard_map/ppermute | solution.py:500
  16.9 0.0 collective-permute-start.3
  16.9 1.5 %early_middle.1 = (f32[1536,256]{1,0:T(8,128)S(1)}, f32[5,8,256]{2,1,0:T(8,128)S(1)}, f32[16,128]{1,0:T(8,128)S(1)}) custom-call(f32[16,128]{1,0:T(8,128)S(1)} %get-tuple-element.70.west_in.west_ref, f32[1536,256]{1,0:T(8,128)S(1)} %get-tuple-element.51.refs_0_, f32[1536,256]{1,0:T(8,128)S(1)} %get-tuple-element.71.refs_1_, ...), custom_call_target="tpu_custom_call" | custom-call | tf_op jit(solution)/shard_map/early_middle/pallas_call | solution.py:441
  18.4 5.4 %collective-permute-start.5 = (f32[16,128]{1,0:T(8,128)S(1)}, f32[16,128]{1,0:T(8,128)S(1)}, u32[]{:S(2)}, u32[]{:S(2)}) collective-permute-start(f32[16,128]{1,0:T(8,128)S(1)} %get-tuple-element.89), channel_id=1, source_target_pairs={{2,0},{4,2},{6,4},{8,6},{10,8},{12,10},{14,12},{16,14},{18,16},{20... | collective-permute-start | bytes 24584 | tf_op jit(solution)/shard_map/ppermute | solution.py:504
  23.8 0.1 late_middle.1
  23.9 0.0 collective-permute-done.4.in_l2
  23.9 0.9 %collective-permute-done.3.from_w = f32[16,128]{1,0:T(8,128)S(1)} collective-permute-done((f32[16,128]{1,0:T(8,128)S(1)}, f32[16,128]{1,0:T(8,128)S(1)}, u32[]{:S(2)}, u32[]{:S(2)}) %collective-permute-start.3) | collective-permute-done | bytes 8224 | tf_op jit(solution)/shard_map/ppermute | solution.py:499
  24.9 0.7 %sums.1 = (f32[128,128]{1,0:T(8,128)}, f32[16,128]{1,0:T(8,128)S(1)}, f32[8,256]{1,0:T(8,128)S(1)}) custom-call(f32[5,8,256]{2,1,0:T(8,128)S(1)} %get-tuple-element.79.sums_in.sums_ref, f32[16,128]{1,0:T(8,128)S(1)} %get-tuple-element.80.east_ref, f32[16,128]{1,0:T(8,128)S(1)} %get-tuple-element.70.west_in.west_ref, f32[32,128]{1,0:T(8,128)S(1)} %get-tuple-element.66.to_e, ...), custom_call_target="tpu_custom_call" | custom-call | tf_op jit(solution)/shard_map/sums/pallas_call | solution.py:441
  25.6 4.6 %all-to-all-start = ((f32[128,1,128]{2,1,0:T(1,128)}), f32[128,1,128]{2,1,0:T(1,128)S(1)}, u32[]{:S(2)}, u32[]{:S(2)}) async-start(f32[128,1,128]{2,1,0:T(1,128)} %bitcast.3), calls=%async_computation | async-start | bytes 131072 | tf_op jit(solution)/shard_map/all_to_all | solution.py:510
  30.2 0.0 collective-permute-done.5.from_e
  30.2 4.2 %outer.1 = (bf16[1536,256]{1,0:T(8,128)(2,1)S(1)}, f32[8,128]{1,0:T(8,128)S(1)}) custom-call(bf16[12,2,128,128]{3,2,1,0:T(8,128)(2,1)} %bitcast.8, bf16[12,2,128,128]{3,2,1,0:T(8,128)(2,1)} %bitcast.10, bf16[1536,256]{1,0:T(8,128)(2,1)} %ef_hbm.3, bf16[1536,256]{1,0:T(8,128)(2,1)} %nf_hbm.3, f32[1536,256]{1,0:T(8,128)S(1)} %get-tuple-element.87.w_ref, ...), custom_call_target="tpu_custom_call" | custom-call | flops 99999997952 | tf_op jit(solution)/shard_map/outer/pallas_call | solution.py:441
  34.5 5.2 %all-to-all-done = f32[128,1,128]{2,1,0:T(1,128)S(1)} async-done(((f32[128,1,128]{2,1,0:T(1,128)}), f32[128,1,128]{2,1,0:T(1,128)S(1)}, u32[]{:S(2)}, u32[]{:S(2)}) %all-to-all-start) | async-done | bytes 65568 | tf_op jit(solution)/shard_map/all_to_all | solution.py:510
  39.6 1.7 %last.1 = (f32[1536,256]{1,0:T(8,128)}, bf16[1536,256]{1,0:T(8,128)(2,1)}) custom-call(f32[128,128]{1,0:T(8,128)S(1)} %bitcast.6, bf16[1536,256]{1,0:T(8,128)(2,1)S(1)} %get-tuple-element.86.z_ref, f32[1536,256]{1,0:T(8,128)S(1)} %get-tuple-element.87.w_ref, bf16[1536,256]{1,0:T(8,128)(2,1)S(1)} %get-tuple-element.92.u_ref, ...), custom_call_target="tpu_custom_call" | custom-call | tf_op jit(solution)/shard_map/last/pallas_call | solution.py:441
  (1 shorter events, 0.0 us)
Async XLA Ops:
  5.5 9.7 %collective-permute-start.1 = (f32[32,128]{1,0:T(8,128)S(1)}, f32[32,128]{1,0:T(8,128)S(1)}, u32[]{:S(2)}, u32[]{:S(2)}) collective-permute-start(f32[32,128]{1,0:T(8,128)S(1)} %get-tuple-element.68), channel_id=1, source_target_pairs={{0,2},{4,6},{8,10},{12,14},{16,18},{20,22},{24,26},{28,30},{32,34}... | collective-permute-start | bytes 49160 | tf_op jit(solution)/shard_map/ppermute | solution.py:488
  5.9 9.3 %collective-permute-start.2 = (f32[32,128]{1,0:T(8,128)S(1)}, f32[32,128]{1,0:T(8,128)S(1)}, u32[]{:S(2)}, u32[]{:S(2)}) collective-permute-start(f32[32,128]{1,0:T(8,128)S(1)} %get-tuple-element.69), channel_id=1, source_target_pairs={{2,4},{6,8},{10,12},{14,16},{18,20},{22,24},{26,28},{30,32},{34,36... | collective-permute-start | bytes 49160 | tf_op jit(solution)/shard_map/ppermute | solution.py:489
  12.8 2.1 %collective-permute-start = (f32[8,256]{1,0:T(8,128)S(1)}, f32[8,256]{1,0:T(8,128)S(1)}, u32[]{:S(2)}, u32[]{:S(2)}) collective-permute-start(f32[8,256]{1,0:T(8,128)S(1)} %get-tuple-element.58.to_l.own_l), channel_id=1, source_target_pairs={{0,1},{1,0},{2,3},{3,2},{4,5},{5,4},{6,7},{7,6},{8,9},{9,8},{10,11... | collective-permute-start | bytes 24584 | tf_op jit(solution)/shard_map/ppermute | solution.py:490
  15.8 8.2 %collective-permute-start.4 = (f32[8,256]{1,0:T(8,128)S(1)}, f32[8,256]{1,0:T(8,128)S(1)}, u32[]{:S(2)}, u32[]{:S(2)}) collective-permute-start(f32[8,256]{1,0:T(8,128)S(1)} %get-tuple-element.84.own_l2), channel_id=1, source_target_pairs={{0,1},{1,0},{2,3},{3,2},{4,5},{5,4},{6,7},{7,6},{8,9},{9,8},{10,11... | collective-permute-start | bytes 24584 | tf_op jit(solution)/shard_map/ppermute | solution.py:500
  16.9 7.9 %collective-permute-start.3 = (f32[16,128]{1,0:T(8,128)S(1)}, f32[16,128]{1,0:T(8,128)S(1)}, u32[]{:S(2)}, u32[]{:S(2)}) collective-permute-start(f32[16,128]{1,0:T(8,128)S(1)} %get-tuple-element.80.east_ref), channel_id=1, source_target_pairs={{0,2},{2,4},{4,6},{6,8},{8,10},{10,12},{12,14},{14,16},{16,18},{18... | collective-permute-start | bytes 24584 | tf_op jit(solution)/shard_map/ppermute | solution.py:499
  18.4 11.8 %collective-permute-start.5 = (f32[16,128]{1,0:T(8,128)S(1)}, f32[16,128]{1,0:T(8,128)S(1)}, u32[]{:S(2)}, u32[]{:S(2)}) collective-permute-start(f32[16,128]{1,0:T(8,128)S(1)} %get-tuple-element.89), channel_id=1, source_target_pairs={{2,0},{4,2},{6,4},{8,6},{10,8},{12,10},{14,12},{16,14},{18,16},{20... | collective-permute-start | bytes 24584 | tf_op jit(solution)/shard_map/ppermute | solution.py:504
  25.6 14.0 %all-to-all-start = ((f32[128,1,128]{2,1,0:T(1,128)}), f32[128,1,128]{2,1,0:T(1,128)S(1)}, u32[]{:S(2)}, u32[]{:S(2)}) async-start(f32[128,1,128]{2,1,0:T(1,128)} %bitcast.3), calls=%async_computation | async-start | bytes 131072 | tf_op jit(solution)/shard_map/all_to_all | solution.py:510

commit v2 on v1

--- a/solution.py
+++ b/solution.py
@@ -13,7 +13,7 @@
 F32 = jnp.float32
 BF16 = jnp.bfloat16
 VMEM_LIMIT = 8 * 1024 * 1024
-HEAD = 6
+HEAD = 5
 SPAN = 16
 ROWS = 16
 
@@ -124,7 +124,7 @@
 
 def first_kernel(
     wet_hbm, rhs_hbm, left_hbm, right_hbm, ef_hbm, nf_hbm,
-    z_ref, short_ref, rhs_ref, left_ref, right_ref, ef_ref, nf_ref, wet_ref, to_e, to_w, to_a, to_b, to_l, sum_ref,
+    short_ref, rhs_ref, left_ref, right_ref, ef_ref, nf_ref, wet_ref, to_e, to_w, to_a, to_b, to_l,
     list_ref, flags_ref, sems,
 ):
     tile_rows = rhs_hbm.shape[0] // EDGE
@@ -157,7 +157,6 @@
     lane = lane_index(1, CELLS)
     for i in range(tile_rows):
         wet_ref[i : i + 1, :] = jnp.where(lane < EDGE, flags_ref[2 * i], flags_ref[2 * i + 1])
-    sums = jnp.zeros(sum_ref.shape, F32)
     for i in range(tile_rows):
         for copy in loads.get(i, ()):
             copy.wait()
@@ -169,19 +168,17 @@
         ]
         short = jnp.concatenate(parts, axis=1)
         short_ref[rows, :] = short
-        precond = short.astype(F32)
-        z_ref[rows, :] = precond
-        edge_rows(i, precond, to_e, to_w)
-        sums = sums + fold(residual * precond)
-    sum_ref[...] = sums
+        to_w[i : i + 1, :] = parts[0].T[0:16, :].astype(F32)[0:1, :]
+        to_e[i : i + 1, :] = parts[1].T[EDGE - 16 :, :].astype(F32)[15:16, :]
     for copy in faces:
         copy.wait()
     for i in range(tile_rows):
-        face = ef_ref[i * EDGE : (i + 1) * EDGE, EDGE:].astype(F32).T[EDGE - 1 :, :]
+        face = ef_ref[i * EDGE : (i + 1) * EDGE, EDGE:].T[EDGE - 16 :, :].astype(F32)[15:16, :]
         to_e[ROWS + i : ROWS + i + 1, :] = face * wet_ref[i : i + 1, EDGE:]
     to_w[ROWS : ROWS + tile_rows, :] = wet_ref[:tile_rows, :EDGE]
-    to_l[0:1, :] = boundary_row(z_ref)
     rows = tile_rows * EDGE
+    upper, lower = short_ref[rows - 16 : rows, :].astype(F32), short_ref[0:16, :].astype(F32)
+    to_l[0:1, :] = jnp.where(on_low_band(), upper[15:16, :], lower[0:1, :])
     last = nf_ref[rows - 16 : rows, :].astype(F32)[15:16, :] * wet_ref[tile_rows - 1 : tile_rows, :]
     to_l[1:2, :] = jnp.where(on_low_band(), last, wet_ref[0:1, :])
     odd = on_odd_sector()
@@ -189,11 +186,12 @@
     to_b[...] = jnp.where(odd, to_w[...], to_e[...])
 
 
-def inner(z_ref, left_ref, right_ref, ef_ref, nf_ref, wet_ref, q_ref, w_ref, east_ref, west_ref):
+def inner(short_ref, left_ref, right_ref, ef_ref, nf_ref, wet_ref, q_ref, w_ref, east_ref, west_ref, z_ref):
     tile_rows = z_ref.shape[0] // EDGE
     east_ref[...] = jnp.zeros_like(east_ref)
     west_ref[...] = jnp.zeros_like(west_ref)
     south = top = jnp.zeros((1, CELLS), F32)
+    z_ref[...] = short_ref[...].astype(F32)
     for i in range(tile_rows):
         rows = slice(i * EDGE, (i + 1) * EDGE)
         _, image, south = stencil(i, tile_rows, z_ref, ef_ref, nf_ref, wet_ref, south, top)
@@ -207,13 +205,13 @@
 
 
 def early_inner_kernel(a_in, b_in, *refs):
-    *arrays, to_a, to_b = refs
+    *arrays, to_a, to_b, z_ref = refs
     to_a[...] = a_in[...]
     to_b[...] = b_in[...]
 
     @pl.when(held_up())
     def _():
-        inner(*arrays)
+        inner(*arrays, z_ref)
 
 
 def late_inner_kernel(*refs):
@@ -284,13 +282,13 @@
 
 
 def middle(
-    z_ref, rhs_ref, q_ref, w_in, ef_ref, nf_ref, wet_ref, lat_ref, turn_e, turn_w, right_e, right_w, sum_in, w_ref, sums_ref
+    z_ref, rhs_ref, q_ref, w_in, ef_ref, nf_ref, wet_ref, lat_ref, turn_e, turn_w, right_e, right_w, w_ref, sums_ref
 ):
     tile_rows = z_ref.shape[0] // EDGE
     zero = jnp.zeros((8, CELLS), F32)
-    zq, rw, qw, faces, squares = zero, zero, zero, zero, zero
-
-    def complete(i, zq, rw, qw):
+    rz, zq, rw, qw, faces, squares = zero, zero, zero, zero, zero, zero
+
+    def complete(i, rz, zq, rw, qw):
         rows = slice(i * EDGE, (i + 1) * EDGE)
         image = q_ref[rows, :]
         product = w_in[rows, :] + jnp.concatenate(
@@ -302,12 +300,14 @@
             by_col = [jnp.broadcast_to(lat_ref[0:1, k * EDGE : (k + 1) * EDGE], (EDGE, EDGE)).T for k in range(2)]
             product = product + jnp.concatenate(by_col, axis=1) * by_row
         w_ref[rows, :] = product
-        return zq + fold(z_ref[rows, :] * image), rw + fold(rhs_ref[rows, :] * product), qw + fold(image * product)
-
-    zq, rw, qw = complete(0, zq, rw, qw)
+        precond, given = z_ref[rows, :].astype(F32), rhs_ref[rows, :]
+        rz, zq = rz + fold(given * precond), zq + fold(precond * image)
+        return rz, zq, rw + fold(given * product), qw + fold(image * product)
+
+    rz, zq, rw, qw = complete(0, rz, zq, rw, qw)
     for i in range(tile_rows):
         if i + 1 < tile_rows:
-            zq, rw, qw = complete(i + 1, zq, rw, qw)
+            rz, zq, rw, qw = complete(i + 1, rz, zq, rw, qw)
         rows = slice(i * EDGE, (i + 1) * EDGE)
         field, over_e, over_n, east_wet, north_wet = differences(i, tile_rows, w_ref, wet_ref)
         by_e = ef_ref[rows, :].astype(F32) * east_wet * (over_e * over_e)
@@ -315,7 +315,7 @@
         by_n = set_row(by_n, -1, 0.0 if i == tile_rows - 1 else by_n[EDGE - 1 :, :] * north_wet)
         faces = faces + fold(by_e + by_n)
         squares = squares + fold(field * field)
-    for k, total in enumerate((sum_in[...], zq, rw, qw, faces + surface_term * squares)):
+    for k, total in enumerate((rz, zq, rw, qw, faces + surface_term * squares)):
         sums_ref[k] = total
 
 
@@ -473,22 +473,23 @@
         pltpu.with_memory_space_constraint(a, pltpu.HBM)
         for a in (wet_list, right_side, left_factor, right_factor, east_face, north_face)
     ]
-    z, short, rhs, left, right, ef, nf, wet, to_e, to_w, to_a, to_b, to_l, rz = call(
+    short, rhs, left, right, ef, nf, wet, to_e, to_w, to_a, to_b, to_l = call(
         first_kernel,
-        [field, half, field, like(left_factor), like(right_factor), like(east_face), like(north_face),
-         shape((ROWS, cols)), message, message, message, message, strip, strip],
+        [half, field, like(left_factor), like(right_factor), like(east_face), like(north_face),
+         shape((ROWS, cols)), message, message, message, message, strip],
         arguments, "first",
         [pltpu.SMEM(wet_list.shape, jnp.int32), pltpu.SMEM((32,), F32),
          pltpu.SemaphoreType.DMA((9,))],
         in_space=pltpu.HBM,
     )
-    arrays = (z, left, right, ef, nf, wet)
+    arrays = (short, left, right, ef, nf, wet)
+    wide = [pltpu.VMEM((rows, cols), F32)]
     results = [field, field, edge, edge]
-    *early, far_a, far_b = call(early_inner_kernel, results + [message, message], (to_a, to_b, *arrays), "early_inner")
+    *early, far_a, far_b = call(early_inner_kernel, results + [message, message], (to_a, to_b, *arrays), "early_inner", wide)
     in_b = lax.ppermute(far_b, "lon", pairs(0))
     in_a = lax.ppermute(far_a, "lon", pairs(1))
     in_l = lax.ppermute(to_l, "lat", across)
-    late = call(late_inner_kernel, results, arrays, "late_inner")
+    late = call(late_inner_kernel, results, arrays, "late_inner", wide)
     lat, row_e, row_w = call(
         lat_kernel, [strip, edge, edge], (early[1], late[1], left, right, to_l, in_l), "lat"
     )
@@ -499,10 +500,10 @@
     from_w2 = lax.ppermute(east, "lon", [(i, (i + 1) % lons) for i in range(lons)])
     in_l2 = lax.ppermute(to_l2, "lat", across)
     results = [field, shape((5, 8, cols))]
-    faces = (ef, nf, wet, lat, turn_e, turn_w, row_e, row_w, rz)
-    *done, to_w2 = call(early_middle_kernel, results + [edge], (west, z, rhs, *early[:2], *faces), "early_middle")
+    faces = (ef, nf, wet, lat, turn_e, turn_w, row_e, row_w)
+    *done, to_w2 = call(early_middle_kernel, results + [edge], (west, short, rhs, *early[:2], *faces), "early_middle")
     from_e2 = lax.ppermute(to_w2, "lon", [((i + 1) % lons, i) for i in range(lons)])
-    w, sums = call(late_middle_kernel, results, (*done, z, rhs, *late[:2], *faces), "late_middle")
+    w, sums = call(late_middle_kernel, results, (*done, short, rhs, *late[:2], *faces), "late_middle")
     packed, flux_w, flux_l = call(
         sums_kernel, [shape((lons * lats, EDGE)), edge, strip],
         (sums, east, west, to_e, to_w, lat, flux_e1, flux_w1, coef_w, to_l, to_l2, in_l, from_w2, in_l2), "sums",

time: 41.7 us -> 41.6 us (level)
  no operation moved by 1% of the time
where the time goes in v2:
time: 41.6 us; the launch traced here: 41.5 us
  starting transfers between devices  19.5 us (47%)
  Pallas kernels  14.2 us (34%)
  waiting for transfers between devices  6.9 us (17%)
  between operations  0.86 us (2%)
    pallas_call x10, Pallas kernels, call(): pl.pallas_call(kernel, out_shape=outs, in_specs=[pl.BlockSpec(memory_spac...  14.2 us
    ppermute x1, starting transfers between devices, per_device(): in_a = lax.ppermute(far_a, 'lon', pairs(1))  6.89 us
    ppermute x1, starting transfers between devices, per_device(): lax.ppermute(to_w2, 'lon', [((i + 1) % lons, i) for i in range(lons)])  5.27 us
    all_to_all x1, waiting for transfers between devices, per_device(): everyone = lax.all_to_all(packed, ('lon', 'lat'), 0, 0, tiled=True)  5.16 us
    all_to_all x1, starting transfers between devices, per_device(): everyone = lax.all_to_all(packed, ('lon', 'lat'), 0, 0, tiled=True)  4.61 us
    ppermute x1, starting transfers between devices, per_device(): in_l = lax.ppermute(to_l, 'lat', across)  1.24 us
    ppermute x1, starting transfers between devices, per_device(): in_l2 = lax.ppermute(to_l2, 'lat', across)  1.16 us
    ppermute x1, waiting for transfers between devices, per_device(): lax.ppermute(east, 'lon', [(i, (i + 1) % lons) for i in range(lons)])  0.91 us
  transfers between devices with their start and end apart: 7, of which 3 were waited for; matrix products, arithmetic and copies ran while one was open for 0% of the time, Pallas kernels for 17%

profile of v2, /device:TPU:1, one launch (start us, length us, event | category | flops | bytes accessed | tf_op | source)
XLA Modules:
  0.0 41.5 jit_solution(3369779324711971190)
XLA Ops:
  0.6 2.6 %first.1 = (bf16[1536,256]{1,0:T(8,128)(2,1)S(1)}, f32[1536,256]{1,0:T(8,128)S(1)}, bf16[12,2,128,128]{3,2,1,0:T(8,128)(2,1)S(1)}, bf16[12,2,128,128]{3,2,1,0:T(...) custom-call(s32[1,24]{1,0:T(1,128)} %wet_hbm.1, ...), custom_call_target="tpu_custom_call" | custom-call | tf_op jit(solution)/shard_map/first/pallas_call | solution.py:441
  3.3 2.2 %early_inner.1 = (f32[1536,256]{1,0:T(8,128)S(1)}, f32[1536,256]{1,0:T(8,128)S(1)}, f32[16,128]{1,0:T(8,128)S(1)}, f32[16,128]{1,0:T(8,128)S(1)}, f32[32,128]{1,0:T(8,128)S(1)}, /*index=5*/f32[32,128]{1,0:T(8,128)S(1)}) custom-call(f32[32,128]{1,0:T(8,128)S(1)} %get-tuple-element.47.a_in, f32[32,128]{1,0:T(8,128)S(1)} %get-tuple-element.48.b_in, ...), custom_call_target="tpu_custom_call" | custom-call | tf_op jit(solution)/shard_map/early_inner/pallas_call | solution.py:441
  5.5 0.4 collective-permute-start.1
  5.9 6.9 %collective-permute-start.2 = (f32[32,128]{1,0:T(8,128)S(1)}, f32[32,128]{1,0:T(8,128)S(1)}, u32[]{:S(2)}, u32[]{:S(2)}) collective-permute-start(f32[32,128]{1,0:T(8,128)S(1)} %get-tuple-element.67), channel_id=1, source_target_pairs={{2,4},{6,8},{10,12},{14,16},{18,20},{22,24},{26,28},{30,32},{34,36... | collective-permute-start | bytes 49160 | tf_op jit(solution)/shard_map/ppermute | solution.py:490
  12.7 1.2 %collective-permute-start = (f32[8,256]{1,0:T(8,128)S(1)}, f32[8,256]{1,0:T(8,128)S(1)}, u32[]{:S(2)}, u32[]{:S(2)}) collective-permute-start(f32[8,256]{1,0:T(8,128)S(1)} %get-tuple-element.56.to_l.own_l), channel_id=1, source_target_pairs={{0,1},{1,0},{2,3},{3,2},{4,5},{5,4},{6,7},{7,6},{8,9},{9,8},{10,11... | collective-permute-start | bytes 24584 | tf_op jit(solution)/shard_map/ppermute | solution.py:491
  14.0 0.8 %collective-permute-done.in_l = f32[8,256]{1,0:T(8,128)S(1)} collective-permute-done((f32[8,256]{1,0:T(8,128)S(1)}, f32[8,256]{1,0:T(8,128)S(1)}, u32[]{:S(2)}, u32[]{:S(2)}) %collective-permute-start) | collective-permute-done | bytes 8224 | tf_op jit(solution)/shard_map/ppermute | solution.py:491
  14.8 0.3 lat.1
  15.1 0.0 collective-permute-done.1.in_b
  15.1 0.0 collective-permute-done.2.in_a
  15.1 0.6 %edges.1 = (f32[16,128]{1,0:T(8,128)S(1)}, f32[16,128]{1,0:T(8,128)S(1)}, f32[16,128]{1,0:T(8,128)S(1)}, f32[16,128]{1,0:T(8,128)S(1)}, f32[16,128]{1,0:T(8,128)...) custom-call(bf16[12,2,128,128]{3,2,1,0:T(8,128)(2,1)S(1)} %get-tuple-element, ...), custom_call_target="tpu_custom_call" | custom-call | tf_op jit(solution)/shard_map/edges/pallas_call | solution.py:441
  15.7 1.2 %collective-permute-start.4 = (f32[8,256]{1,0:T(8,128)S(1)}, f32[8,256]{1,0:T(8,128)S(1)}, u32[]{:S(2)}, u32[]{:S(2)}) collective-permute-start(f32[8,256]{1,0:T(8,128)S(1)} %get-tuple-element.81.own_l2), channel_id=1, source_target_pairs={{0,1},{1,0},{2,3},{3,2},{4,5},{5,4},{6,7},{7,6},{8,9},{9,8},{10,11... | collective-permute-start | bytes 24584 | tf_op jit(solution)/shard_map/ppermute | solution.py:501
  16.9 0.0 collective-permute-start.3
  16.9 1.6 %early_middle.1 = (f32[1536,256]{1,0:T(8,128)S(1)}, f32[5,8,256]{2,1,0:T(8,128)S(1)}, f32[16,128]{1,0:T(8,128)S(1)}) custom-call(f32[16,128]{1,0:T(8,128)S(1)} %get-tuple-element.68.west_in.west_ref, bf16[1536,256]{1,0:T(8,128)(2,1)S(1)} %get-tuple-element.49.refs_0_.z_ref, f32[1536,256]{1,0:T(8,128)S(1)} %get-tuple-element.69.refs_1_, ...), custom_call_target="tpu_custom_call" | custom-call | tf_op jit(solution)/shard_map/early_middle/pallas_call | solution.py:441
  18.5 5.3 %collective-permute-start.5 = (f32[16,128]{1,0:T(8,128)S(1)}, f32[16,128]{1,0:T(8,128)S(1)}, u32[]{:S(2)}, u32[]{:S(2)}) collective-permute-start(f32[16,128]{1,0:T(8,128)S(1)} %get-tuple-element.85), channel_id=1, source_target_pairs={{2,0},{4,2},{6,4},{8,6},{10,8},{12,10},{14,12},{16,14},{18,16},{20... | collective-permute-start | bytes 24584 | tf_op jit(solution)/shard_map/ppermute | solution.py:505
  23.8 0.1 late_middle.1
  23.9 0.0 collective-permute-done.4.in_l2
  23.9 0.9 %collective-permute-done.3.from_w = f32[16,128]{1,0:T(8,128)S(1)} collective-permute-done((f32[16,128]{1,0:T(8,128)S(1)}, f32[16,128]{1,0:T(8,128)S(1)}, u32[]{:S(2)}, u32[]{:S(2)}) %collective-permute-start.3) | collective-permute-done | bytes 8224 | tf_op jit(solution)/shard_map/ppermute | solution.py:500
  24.8 0.7 %sums.1 = (f32[128,128]{1,0:T(8,128)}, f32[16,128]{1,0:T(8,128)S(1)}, f32[8,256]{1,0:T(8,128)S(1)}) custom-call(f32[5,8,256]{2,1,0:T(8,128)S(1)} %get-tuple-element.76.sums_in.sums_ref, f32[16,128]{1,0:T(8,128)S(1)} %get-tuple-element.77.east_ref, f32[16,128]{1,0:T(8,128)S(1)} %get-tuple-element.68.west_in.west_ref, f32[32,128]{1,0:T(8,128)S(1)} %get-tuple-element.64.to_e, ...), custom_call_target="tpu_custom_call" | custom-call | tf_op jit(solution)/shard_map/sums/pallas_call | solution.py:441
  25.5 4.6 %all-to-all-start = ((f32[128,1,128]{2,1,0:T(1,128)}), f32[128,1,128]{2,1,0:T(1,128)S(1)}, u32[]{:S(2)}, u32[]{:S(2)}) async-start(f32[128,1,128]{2,1,0:T(1,128)} %bitcast.3), calls=%async_computation | async-start | bytes 131072 | tf_op jit(solution)/shard_map/all_to_all | solution.py:511
  30.2 0.0 collective-permute-done.5.from_e
  30.2 4.2 %outer.1 = (bf16[1536,256]{1,0:T(8,128)(2,1)S(1)}, f32[8,128]{1,0:T(8,128)S(1)}) custom-call(bf16[12,2,128,128]{3,2,1,0:T(8,128)(2,1)} %bitcast.8, bf16[12,2,128,128]{3,2,1,0:T(8,128)(2,1)} %bitcast.10, bf16[1536,256]{1,0:T(8,128)(2,1)} %ef_hbm.3, bf16[1536,256]{1,0:T(8,128)(2,1)} %nf_hbm.3, f32[1536,256]{1,0:T(8,128)S(1)} %get-tuple-element.83.w_ref, ...), custom_call_target="tpu_custom_call" | custom-call | flops 99999997952 | tf_op jit(solution)/shard_map/outer/pallas_call | solution.py:441
  34.4 5.2 %all-to-all-done = f32[128,1,128]{2,1,0:T(1,128)S(1)} async-done(((f32[128,1,128]{2,1,0:T(1,128)}), f32[128,1,128]{2,1,0:T(1,128)S(1)}, u32[]{:S(2)}, u32[]{:S(2)}) %all-to-all-start) | async-done | bytes 65568 | tf_op jit(solution)/shard_map/all_to_all | solution.py:511
  39.6 1.7 %last.1 = (f32[1536,256]{1,0:T(8,128)}, bf16[1536,256]{1,0:T(8,128)(2,1)}) custom-call(f32[128,128]{1,0:T(8,128)S(1)} %bitcast.6, bf16[1536,256]{1,0:T(8,128)(2,1)S(1)} %get-tuple-element.49.refs_0_.z_ref, f32[1536,256]{1,0:T(8,128)S(1)} %get-tuple-element.83.w_ref, bf16[1536,256]{1,0:T(8,128)(2,1)S(1)} %get-tuple-element.88.u_ref, ...), custom_call_target="tpu_custom_call" | custom-call | tf_op jit(solution)/shard_map/last/pallas_call | solution.py:441
  (1 shorter events, 0.0 us)
Async XLA Ops:
  5.5 9.6 %collective-permute-start.1 = (f32[32,128]{1,0:T(8,128)S(1)}, f32[32,128]{1,0:T(8,128)S(1)}, u32[]{:S(2)}, u32[]{:S(2)}) collective-permute-start(f32[32,128]{1,0:T(8,128)S(1)} %get-tuple-element.66), channel_id=1, source_target_pairs={{0,2},{4,6},{8,10},{12,14},{16,18},{20,22},{24,26},{28,30},{32,34}... | collective-permute-start | bytes 49160 | tf_op jit(solution)/shard_map/ppermute | solution.py:489
  5.9 9.3 %collective-permute-start.2 = (f32[32,128]{1,0:T(8,128)S(1)}, f32[32,128]{1,0:T(8,128)S(1)}, u32[]{:S(2)}, u32[]{:S(2)}) collective-permute-start(f32[32,128]{1,0:T(8,128)S(1)} %get-tuple-element.67), channel_id=1, source_target_pairs={{2,4},{6,8},{10,12},{14,16},{18,20},{22,24},{26,28},{30,32},{34,36... | collective-permute-start | bytes 49160 | tf_op jit(solution)/shard_map/ppermute | solution.py:490
  12.7 2.1 %collective-permute-start = (f32[8,256]{1,0:T(8,128)S(1)}, f32[8,256]{1,0:T(8,128)S(1)}, u32[]{:S(2)}, u32[]{:S(2)}) collective-permute-start(f32[8,256]{1,0:T(8,128)S(1)} %get-tuple-element.56.to_l.own_l), channel_id=1, source_target_pairs={{0,1},{1,0},{2,3},{3,2},{4,5},{5,4},{6,7},{7,6},{8,9},{9,8},{10,11... | collective-permute-start | bytes 24584 | tf_op jit(solution)/shard_map/ppermute | solution.py:491
  15.7 8.2 %collective-permute-start.4 = (f32[8,256]{1,0:T(8,128)S(1)}, f32[8,256]{1,0:T(8,128)S(1)}, u32[]{:S(2)}, u32[]{:S(2)}) collective-permute-start(f32[8,256]{1,0:T(8,128)S(1)} %get-tuple-element.81.own_l2), channel_id=1, source_target_pairs={{0,1},{1,0},{2,3},{3,2},{4,5},{5,4},{6,7},{7,6},{8,9},{9,8},{10,11... | collective-permute-start | bytes 24584 | tf_op jit(solution)/shard_map/ppermute | solution.py:501
  16.9 7.9 %collective-permute-start.3 = (f32[16,128]{1,0:T(8,128)S(1)}, f32[16,128]{1,0:T(8,128)S(1)}, u32[]{:S(2)}, u32[]{:S(2)}) collective-permute-start(f32[16,128]{1,0:T(8,128)S(1)} %get-tuple-element.77.east_ref), channel_id=1, source_target_pairs={{0,2},{2,4},{4,6},{6,8},{8,10},{10,12},{12,14},{14,16},{16,18},{18... | collective-permute-start | bytes 24584 | tf_op jit(solution)/shard_map/ppermute | solution.py:500
  18.5 11.7 %collective-permute-start.5 = (f32[16,128]{1,0:T(8,128)S(1)}, f32[16,128]{1,0:T(8,128)S(1)}, u32[]{:S(2)}, u32[]{:S(2)}) collective-permute-start(f32[16,128]{1,0:T(8,128)S(1)} %get-tuple-element.85), channel_id=1, source_target_pairs={{2,0},{4,2},{6,4},{8,6},{10,8},{12,10},{14,12},{16,14},{18,16},{20... | collective-permute-start | bytes 24584 | tf_op jit(solution)/shard_map/ppermute | solution.py:505
  25.5 14.0 %all-to-all-start = ((f32[128,1,128]{2,1,0:T(1,128)}), f32[128,1,128]{2,1,0:T(1,128)S(1)}, u32[]{:S(2)}, u32[]{:S(2)}) async-start(f32[128,1,128]{2,1,0:T(1,128)} %bitcast.3), calls=%async_computation | async-start | bytes 131072 | tf_op jit(solution)/shard_map/all_to_all | solution.py:511

commit v3 on v2

--- a/solution.py
+++ b/solution.py
@@ -13,7 +13,7 @@
 F32 = jnp.float32
 BF16 = jnp.bfloat16
 VMEM_LIMIT = 8 * 1024 * 1024
-HEAD = 5
+HEAD = 4
 SPAN = 16
 ROWS = 16
 
@@ -267,10 +267,12 @@
 
 def edge_kernel(
     left_ref, lat_ref, row_e, row_w, early_e, late_e, early_w, late_w, to_e, to_w, in_b, in_a,
-    east_ref, coef_e, flux_e, turn_e, west_ref, coef_w, flux_w, turn_w, to_l2,
+    east_ref, coef_e, flux_e, turn_e, west_ref, coef_w, flux_w, turn_w, to_l2, send_e,
 ):
     one_side(1, left_ref, lat_ref, row_e, early_e, late_e, to_e, in_b, in_a, east_ref, coef_e, flux_e, turn_e)
     one_side(0, left_ref, lat_ref, row_w, early_w, late_w, to_w, in_b, in_a, west_ref, coef_w, flux_w, turn_w)
+    send_e[...] = jnp.zeros_like(send_e)
+    send_e[:ROWS, :] = east_ref[...]
     end = left_ref.shape[0] - 1
     low = on_low_band()
     by_lon = [
@@ -346,7 +348,7 @@
     sums_in, east_ref, west_ref, to_e, to_w, lat_ref, flux_e1, flux_w1, coef_w, own_l, own_l2, in_l, from_w, in_l2,
     packed_ref, flux_w, flux_l,
 ):
-    over_w = west_ref[...] - from_w[...]
+    over_w = west_ref[...] - from_w[:ROWS, :]
     flux_w[...] = coef_w[...] * over_w
     top, bottom = lat_flux(own_l[1:2, :] * in_l[1:2, :], own_l2[0:1, :], in_l2[0:1, :])
     flux_l[...] = jnp.zeros_like(flux_l)
@@ -493,11 +495,11 @@
     lat, row_e, row_w = call(
         lat_kernel, [strip, edge, edge], (early[1], late[1], left, right, to_l, in_l), "lat"
     )
-    east, coef_e, flux_e1, turn_e, west, coef_w, flux_w1, turn_w, to_l2 = call(
-        edge_kernel, [edge] * 8 + [strip],
+    east, coef_e, flux_e1, turn_e, west, coef_w, flux_w1, turn_w, to_l2, send_e = call(
+        edge_kernel, [edge] * 8 + [strip, message],
         (left, lat, row_e, row_w, early[2], late[2], early[3], late[3], to_e, to_w, in_b, in_a), "edges",
     )
-    from_w2 = lax.ppermute(east, "lon", [(i, (i + 1) % lons) for i in range(lons)])
+    from_w2 = lax.ppermute(send_e, "lon", [(i, (i + 1) % lons) for i in range(lons)])
     in_l2 = lax.ppermute(to_l2, "lat", across)
     results = [field, shape((5, 8, cols))]
     faces = (ef, nf, wet, lat, turn_e, turn_w, row_e, row_w)

time: 41.6 us -> 41.7 us (level)
  waiting for transfers between devices: 6.9 us -> 6 us
  starting transfers between devices: 19.5 us -> 20.4 us
    ppermute x1, waiting for transfers between devices: 0.91 us -> 0.01 us  [per_device(): lax.ppermute(send_e, 'lon', [(i, (i + 1) % lons) for i in range(lons)])]
    all_to_all x1, starting transfers between devices: 4.61 us -> 5.24 us  [per_device(): everyone = lax.all_to_all(packed, ('lon', 'lat'), 0, 0, tiled=True)]
  transfers between devices with their start and end apart: 7 -> 7, of which waited for: 3 -> 2; matrix products, arithmetic and copies ran while one was open for 0% -> 0% of each run, Pallas kernels for 17% -> 17%
where the time goes in v3:
time: 41.7 us; the launch traced here: 41.5 us
  starting transfers between devices  20.4 us (49%)
  Pallas kernels  14.2 us (34%)
  waiting for transfers between devices  6 us (14%)
  between operations  0.88 us (2%)
    pallas_call x10, Pallas kernels, call(): pl.pallas_call(kernel, out_shape=outs, in_specs=[pl.BlockSpec(memory_spac...  14.2 us
    ppermute x1, starting transfers between devices, per_device(): in_a = lax.ppermute(far_a, 'lon', pairs(1))  6.89 us
    ppermute x1, starting transfers between devices, per_device(): lax.ppermute(to_w2, 'lon', [((i + 1) % lons, i) for i in range(lons)])  5.44 us
    all_to_all x1, starting transfers between devices, per_device(): everyone = lax.all_to_all(packed, ('lon', 'lat'), 0, 0, tiled=True)  5.24 us
    all_to_all x1, waiting for transfers between devices, per_device(): everyone = lax.all_to_all(packed, ('lon', 'lat'), 0, 0, tiled=True)  5.16 us
    ppermute x1, starting transfers between devices, per_device(): in_l = lax.ppermute(to_l, 'lat', across)  1.23 us
    ppermute x1, starting transfers between devices, per_device(): in_l2 = lax.ppermute(to_l2, 'lat', across)  1.17 us
  transfers between devices with their start and end apart: 7, of which 2 were waited for; matrix products, arithmetic and copies ran while one was open for 0% of the time, Pallas kernels for 17%

profile of v3, /device:TPU:1, one launch (start us, length us, event | category | flops | bytes accessed | tf_op | source)
XLA Modules:
  0.0 41.5 jit_solution(15788871648382582222)
XLA Ops:
  0.6 2.7 %first.1 = (bf16[1536,256]{1,0:T(8,128)(2,1)S(1)}, f32[1536,256]{1,0:T(8,128)S(1)}, bf16[12,2,128,128]{3,2,1,0:T(8,128)(2,1)S(1)}, bf16[12,2,128,128]{3,2,1,0:T(...) custom-call(s32[1,24]{1,0:T(1,128)} %wet_hbm.1, ...), custom_call_target="tpu_custom_call" | custom-call | tf_op jit(solution)/shard_map/first/pallas_call | solution.py:443
  3.3 2.2 %early_inner.1 = (f32[1536,256]{1,0:T(8,128)S(1)}, f32[1536,256]{1,0:T(8,128)S(1)}, f32[16,128]{1,0:T(8,128)S(1)}, f32[16,128]{1,0:T(8,128)S(1)}, f32[32,128]{1,0:T(8,128)S(1)}, /*index=5*/f32[32,128]{1,0:T(8,128)S(1)}) custom-call(f32[32,128]{1,0:T(8,128)S(1)} %get-tuple-element.48.a_in, f32[32,128]{1,0:T(8,128)S(1)} %get-tuple-element.49.b_in, ...), custom_call_target="tpu_custom_call" | custom-call | tf_op jit(solution)/shard_map/early_inner/pallas_call | solution.py:443
  5.5 0.4 collective-permute-start.1
  5.9 6.9 %collective-permute-start.2 = (f32[32,128]{1,0:T(8,128)S(1)}, f32[32,128]{1,0:T(8,128)S(1)}, u32[]{:S(2)}, u32[]{:S(2)}) collective-permute-start(f32[32,128]{1,0:T(8,128)S(1)} %get-tuple-element.68), channel_id=1, source_target_pairs={{2,4},{6,8},{10,12},{14,16},{18,20},{22,24},{26,28},{30,32},{34,36... | collective-permute-start | bytes 49160 | tf_op jit(solution)/shard_map/ppermute | solution.py:492
  12.8 1.2 %collective-permute-start = (f32[8,256]{1,0:T(8,128)S(1)}, f32[8,256]{1,0:T(8,128)S(1)}, u32[]{:S(2)}, u32[]{:S(2)}) collective-permute-start(f32[8,256]{1,0:T(8,128)S(1)} %get-tuple-element.57.to_l.own_l), channel_id=1, source_target_pairs={{0,1},{1,0},{2,3},{3,2},{4,5},{5,4},{6,7},{7,6},{8,9},{9,8},{10,11... | collective-permute-start | bytes 24584 | tf_op jit(solution)/shard_map/ppermute | solution.py:493
  14.0 0.8 %collective-permute-done.in_l = f32[8,256]{1,0:T(8,128)S(1)} collective-permute-done((f32[8,256]{1,0:T(8,128)S(1)}, f32[8,256]{1,0:T(8,128)S(1)}, u32[]{:S(2)}, u32[]{:S(2)}) %collective-permute-start) | collective-permute-done | bytes 8224 | tf_op jit(solution)/shard_map/ppermute | solution.py:493
  14.9 0.3 lat.1
  15.2 0.0 collective-permute-done.1.in_b
  15.2 0.0 collective-permute-done.2.in_a
  15.2 0.6 %edges.1 = (f32[16,128]{1,0:T(8,128)S(1)}, f32[16,128]{1,0:T(8,128)S(1)}, f32[16,128]{1,0:T(8,128)S(1)}, f32[16,128]{1,0:T(8,128)S(1)}, f32[16,128]{1,0:T(8,128)...) custom-call(bf16[12,2,128,128]{3,2,1,0:T(8,128)(2,1)S(1)} %get-tuple, ...), custom_call_target="tpu_custom_call" | custom-call | tf_op jit(solution)/shard_map/edges/pallas_call | solution.py:443
  15.7 0.1 collective-permute-start.3
  15.8 1.2 %collective-permute-start.4 = (f32[8,256]{1,0:T(8,128)S(1)}, f32[8,256]{1,0:T(8,128)S(1)}, u32[]{:S(2)}, u32[]{:S(2)}) collective-permute-start(f32[8,256]{1,0:T(8,128)S(1)} %get-tuple-element.82.own_l2), channel_id=1, source_target_pairs={{0,1},{1,0},{2,3},{3,2},{4,5},{5,4},{6,7},{7,6},{8,9},{9,8},{10,11... | collective-permute-start | bytes 24584 | tf_op jit(solution)/shard_map/ppermute | solution.py:503
  17.0 1.6 %early_middle.1 = (f32[1536,256]{1,0:T(8,128)S(1)}, f32[5,8,256]{2,1,0:T(8,128)S(1)}, f32[16,128]{1,0:T(8,128)S(1)}) custom-call(f32[16,128]{1,0:T(8,128)S(1)} %get-tuple-element.69.west_in.west_ref, bf16[1536,256]{1,0:T(8,128)(2,1)S(1)} %get-tuple-element.50.refs_0_.z_ref, f32[1536,256]{1,0:T(8,128)S(1)} %get-tuple-element.70.refs_1_, ...), custom_call_target="tpu_custom_call" | custom-call | tf_op jit(solution)/shard_map/early_middle/pallas_call | solution.py:443
  18.6 5.4 %collective-permute-start.5 = (f32[16,128]{1,0:T(8,128)S(1)}, f32[16,128]{1,0:T(8,128)S(1)}, u32[]{:S(2)}, u32[]{:S(2)}) collective-permute-start(f32[16,128]{1,0:T(8,128)S(1)} %get-tuple-element.87), channel_id=1, source_target_pairs={{2,0},{4,2},{6,4},{8,6},{10,8},{12,10},{14,12},{16,14},{18,16},{20... | collective-permute-start | bytes 24584 | tf_op jit(solution)/shard_map/ppermute | solution.py:507
  24.1 0.1 late_middle.1
  24.2 0.0 collective-permute-done.4.in_l2
  24.2 0.0 collective-permute-done.3.from_w
  24.2 0.7 %sums.1 = (f32[128,128]{1,0:T(8,128)}, f32[16,128]{1,0:T(8,128)S(1)}, f32[8,256]{1,0:T(8,128)S(1)}) custom-call(f32[5,8,256]{2,1,0:T(8,128)S(1)} %get-tuple-element.77.sums_in.sums_ref, f32[16,128]{1,0:T(8,128)S(1)} %get-tuple-element.78.east_ref, f32[16,128]{1,0:T(8,128)S(1)} %get-tuple-element.69.west_in.west_ref, f32[32,128]{1,0:T(8,128)S(1)} %get-tuple-element.65.to_e, ...), custom_call_target="tpu_custom_call" | custom-call | tf_op jit(solution)/shard_map/sums/pallas_call | solution.py:443
  24.9 5.2 %all-to-all-start = ((f32[128,1,128]{2,1,0:T(1,128)}), f32[128,1,128]{2,1,0:T(1,128)S(1)}, u32[]{:S(2)}, u32[]{:S(2)}) async-start(f32[128,1,128]{2,1,0:T(1,128)} %bitcast.3), calls=%async_computation | async-start | bytes 131072 | tf_op jit(solution)/shard_map/all_to_all | solution.py:513
  30.2 0.0 collective-permute-done.5.from_e
  30.2 4.2 %outer.1 = (bf16[1536,256]{1,0:T(8,128)(2,1)S(1)}, f32[8,128]{1,0:T(8,128)S(1)}) custom-call(bf16[12,2,128,128]{3,2,1,0:T(8,128)(2,1)} %bitcast.8, bf16[12,2,128,128]{3,2,1,0:T(8,128)(2,1)} %bitcast.10, bf16[1536,256]{1,0:T(8,128)(2,1)} %ef_hbm.3, bf16[1536,256]{1,0:T(8,128)(2,1)} %nf_hbm.3, f32[1536,256]{1,0:T(8,128)S(1)} %get-tuple-element.85.w_ref, ...), custom_call_target="tpu_custom_call" | custom-call | flops 99999997952 | tf_op jit(solution)/shard_map/outer/pallas_call | solution.py:443
  34.5 5.2 %all-to-all-done = f32[128,1,128]{2,1,0:T(1,128)S(1)} async-done(((f32[128,1,128]{2,1,0:T(1,128)}), f32[128,1,128]{2,1,0:T(1,128)S(1)}, u32[]{:S(2)}, u32[]{:S(2)}) %all-to-all-start) | async-done | bytes 65568 | tf_op jit(solution)/shard_map/all_to_all | solution.py:513
  39.6 1.7 %last.1 = (f32[1536,256]{1,0:T(8,128)}, bf16[1536,256]{1,0:T(8,128)(2,1)}) custom-call(f32[128,128]{1,0:T(8,128)S(1)} %bitcast.6, bf16[1536,256]{1,0:T(8,128)(2,1)S(1)} %get-tuple-element.50.refs_0_.z_ref, f32[1536,256]{1,0:T(8,128)S(1)} %get-tuple-element.85.w_ref, bf16[1536,256]{1,0:T(8,128)(2,1)S(1)} %get-tuple-element.90.u_ref, ...), custom_call_target="tpu_custom_call" | custom-call | tf_op jit(solution)/shard_map/last/pallas_call | solution.py:443
  (1 shorter events, 0.0 us)
Async XLA Ops:
  5.5 9.7 %collective-permute-start.1 = (f32[32,128]{1,0:T(8,128)S(1)}, f32[32,128]{1,0:T(8,128)S(1)}, u32[]{:S(2)}, u32[]{:S(2)}) collective-permute-start(f32[32,128]{1,0:T(8,128)S(1)} %get-tuple-element.67), channel_id=1, source_target_pairs={{0,2},{4,6},{8,10},{12,14},{16,18},{20,22},{24,26},{28,30},{32,34}... | collective-permute-start | bytes 49160 | tf_op jit(solution)/shard_map/ppermute | solution.py:491
  5.9 9.3 %collective-permute-start.2 = (f32[32,128]{1,0:T(8,128)S(1)}, f32[32,128]{1,0:T(8,128)S(1)}, u32[]{:S(2)}, u32[]{:S(2)}) collective-permute-start(f32[32,128]{1,0:T(8,128)S(1)} %get-tuple-element.68), channel_id=1, source_target_pairs={{2,4},{6,8},{10,12},{14,16},{18,20},{22,24},{26,28},{30,32},{34,36... | collective-permute-start | bytes 49160 | tf_op jit(solution)/shard_map/ppermute | solution.py:492
  12.8 2.1 %collective-permute-start = (f32[8,256]{1,0:T(8,128)S(1)}, f32[8,256]{1,0:T(8,128)S(1)}, u32[]{:S(2)}, u32[]{:S(2)}) collective-permute-start(f32[8,256]{1,0:T(8,128)S(1)} %get-tuple-element.57.to_l.own_l), channel_id=1, source_target_pairs={{0,1},{1,0},{2,3},{3,2},{4,5},{5,4},{6,7},{7,6},{8,9},{9,8},{10,11... | collective-permute-start | bytes 24584 | tf_op jit(solution)/shard_map/ppermute | solution.py:493
  15.7 8.4 %collective-permute-start.3 = (f32[32,128]{1,0:T(8,128)S(1)}, f32[32,128]{1,0:T(8,128)S(1)}, u32[]{:S(2)}, u32[]{:S(2)}) collective-permute-start(f32[32,128]{1,0:T(8,128)S(1)} %get-tuple-element.83), channel_id=1, source_target_pairs={{0,2},{2,4},{4,6},{6,8},{8,10},{10,12},{12,14},{14,16},{16,18},{18... | collective-permute-start | bytes 49160 | tf_op jit(solution)/shard_map/ppermute | solution.py:502
  15.8 8.4 %collective-permute-start.4 = (f32[8,256]{1,0:T(8,128)S(1)}, f32[8,256]{1,0:T(8,128)S(1)}, u32[]{:S(2)}, u32[]{:S(2)}) collective-permute-start(f32[8,256]{1,0:T(8,128)S(1)} %get-tuple-element.82.own_l2), channel_id=1, source_target_pairs={{0,1},{1,0},{2,3},{3,2},{4,5},{5,4},{6,7},{7,6},{8,9},{9,8},{10,11... | collective-permute-start | bytes 24584 | tf_op jit(solution)/shard_map/ppermute | solution.py:503
  18.6 11.6 %collective-permute-start.5 = (f32[16,128]{1,0:T(8,128)S(1)}, f32[16,128]{1,0:T(8,128)S(1)}, u32[]{:S(2)}, u32[]{:S(2)}) collective-permute-start(f32[16,128]{1,0:T(8,128)S(1)} %get-tuple-element.87), channel_id=1, source_target_pairs={{2,0},{4,2},{6,4},{8,6},{10,8},{12,10},{14,12},{16,14},{18,16},{20... | collective-permute-start | bytes 24584 | tf_op jit(solution)/shard_map/ppermute | solution.py:507
  24.9 14.7 %all-to-all-start = ((f32[128,1,128]{2,1,0:T(1,128)}), f32[128,1,128]{2,1,0:T(1,128)S(1)}, u32[]{:S(2)}, u32[]{:S(2)}) async-start(f32[128,1,128]{2,1,0:T(1,128)} %bitcast.3), calls=%async_computation | async-start | bytes 131072 | tf_op jit(solution)/shard_map/all_to_all | solution.py:513
